TPU v7x, 128 devices: a whole 4x4x4 slice. The times are simulated.
128 devices in a mesh: enc: 16 (over y, x_lo, core), dec: 8 (over x_hi, z).
Axes of the slice: x: 4 (x_hi: 2, x_lo: 2; x = x_hi * 2 + x_lo), y: 4, z: 4, core: 2. Of those that a mesh axis runs over, the one named last changes fastest.
Arguments:
- tokens: bfloat16 [2048, 4096], P('dec'), may hold values from -21 to 21
- w_query: bfloat16 [4096, 4096], P(None, 'enc'), may hold values from -0.09375 to 0.09375
- context: bfloat16 [4096, 1024], P('enc'), may hold values from -6 to 6
- w_key: bfloat16 [1024, 4096], P(None, 'enc'), may hold values from -0.1875 to 0.1875
- w_value: bfloat16 [1024, 4096], P(None, 'enc'), may hold values from -0.1875 to 0.1875
- self_query: bfloat16 [2048, 4096], P('dec', 'enc'), may hold values from -90 to 90
- self_key: bfloat16 [2048, 4096], P('dec', 'enc'), may hold values from -4 to 4
- self_value: bfloat16 [2048, 4096], P('dec', 'enc'), may hold values from -6 to 6
- grad_self: bfloat16 [2048, 4096], P('dec', 'enc'), may hold values from -6 to 6
- grad_cross: bfloat16 [2048, 4096], P('dec', 'enc'), may hold values from -6 to 6
Outputs:
- self_out: bfloat16 [2048, 4096], P('dec', 'enc')
- grad_self_query: float32 [2048, 4096], P('dec', 'enc')
- grad_self_key: float32 [2048, 4096], P('dec', 'enc')
- grad_self_value: float32 [2048, 4096], P('dec', 'enc')
- cross_out: bfloat16 [2048, 4096], P('dec', 'enc')
- grad_w_query: float32 [4096, 4096], P('dec', 'enc')
- grad_w_key: float32 [1024, 4096], P('dec', 'enc')
- grad_w_value: float32 [1024, 4096], P('dec', 'enc')
All inputs are finite; a program needn't handle non-finite values.
Results may differ from a plain program's by a relative error of at most 0.029.
The roundings to bfloat16 on the way count: a program that leaves them out, or rounds other values in their place, can miss the bound.
Values may be sent and summed in bfloat16 or wider, within the bound.
A program may use at most 128 MiB of HBM per device.

v0:
```python
import math

import jax
import jax.numpy as jnp
from jax import lax
from jax.sharding import PartitionSpec as P

HD = 128


def online_update(running, scores, value_block):
    old_max, normaliser, context_sum = running
    new_max = jnp.maximum(old_max, jnp.max(scores, axis=2, keepdims=True))
    weights = jnp.exp(scores - new_max)
    factor = jnp.exp(old_max - new_max)
    normaliser = normaliser * factor + jnp.sum(weights, axis=2, keepdims=True)
    context_sum = context_sum * factor + jnp.einsum(
        "hrk,khd->hrd",
        weights.astype(jnp.bfloat16),
        value_block,
        preferred_element_type=jnp.float32,
    )
    return (new_max, normaliser, context_sum)


def score_grads(scores, log_norm, row_delta, grad_heads, value_block, score_scale):
    probability = jnp.exp(scores - log_norm)
    grad_prob = jnp.einsum(
        "rhd,khd->hrk", grad_heads, value_block, preferred_element_type=jnp.float32
    )
    grad_score = (probability * (grad_prob - row_delta) * score_scale).astype(jnp.bfloat16)
    return (probability, grad_score)


def backward_terms(
    scores, log_norm, row_delta, query_heads, grad_heads, key_block, value_block, score_scale
):
    probability, grad_score = score_grads(
        scores, log_norm, row_delta, grad_heads, value_block, score_scale
    )
    grad_value = jnp.einsum(
        "hrk,rhd->khd",
        probability.astype(jnp.bfloat16),
        grad_heads,
        preferred_element_type=jnp.float32,
    )
    grad_query = jnp.einsum(
        "hrk,khd->hrd", grad_score, key_block, preferred_element_type=jnp.float32
    )
    grad_key = jnp.einsum(
        "hrk,rhd->khd", grad_score, query_heads, preferred_element_type=jnp.float32
    )
    return (grad_query, grad_key, grad_value)


def body(
    tokens,
    w_query,
    context,
    w_key,
    w_value,
    self_query,
    self_key,
    self_value,
    grad_self,
    grad_cross,
):
    tok_rows = tokens.shape[0]
    head_count = self_query.shape[1] // HD
    score_scale = HD ** (-0.5)
    groups = lax.axis_size("dec")
    first_row = lax.axis_index("dec") * tok_rows
    keys_all, values_all = (
        lax.all_gather(self_key, "dec", axis=0, tiled=True),
        lax.all_gather(self_value, "dec", axis=0, tiled=True),
    )
    span_rows = keys_all.shape[0]
    step_rows = tok_rows * math.gcd(groups, max(1, 512 // tok_rows))
    all_blocks = span_rows // step_rows
    query_heads = self_query.reshape(tok_rows, head_count, HD)
    grad_heads = grad_self.reshape(tok_rows, head_count, HD)
    query_place = first_row + lax.broadcasted_iota(jnp.int32, (1, tok_rows, step_rows), 1)

    def scores_for(block_index):
        begin = block_index * step_rows
        key_block = lax.dynamic_slice_in_dim(keys_all, begin, step_rows, 0).reshape(
            step_rows, head_count, HD
        )
        value_block = lax.dynamic_slice_in_dim(values_all, begin, step_rows, 0).reshape(
            step_rows, head_count, HD
        )
        raw_scores = (
            jnp.einsum("rhd,khd->hrk", query_heads, key_block, preferred_element_type=jnp.float32)
            * score_scale
        )
        key_place = begin + lax.broadcasted_iota(jnp.int32, (1, tok_rows, step_rows), 2)
        return (jnp.where(query_place >= key_place, raw_scores, -1e30), key_block, value_block)

    def forward_step(block_index, running):
        scores, key_block, value_block = scores_for(block_index)
        return online_update(running, scores, value_block)

    initial = (
        jnp.full((head_count, tok_rows, 1), -1e30, jnp.float32),
        jnp.zeros((head_count, tok_rows, 1), jnp.float32),
        jnp.zeros((head_count, tok_rows, HD), jnp.float32),
    )
    self_max, self_norm, self_sum = lax.fori_loop(0, all_blocks, forward_step, initial)
    self_context = (self_sum / self_norm).astype(jnp.bfloat16)
    self_log = self_max + jnp.log(self_norm)
    self_delta = jnp.sum(
        grad_heads.astype(jnp.float32).transpose(1, 0, 2) * self_context.astype(jnp.float32),
        axis=2,
        keepdims=True,
    )
    query_zero = jnp.zeros((head_count, tok_rows, HD), jnp.float32)

    def backward_step(block_index, running):
        query_acc, key_buffer, value_buffer = running
        scores, key_block, value_block = scores_for(block_index)
        add_query, grad_key, grad_value = backward_terms(
            scores,
            self_log,
            self_delta,
            query_heads,
            grad_heads,
            key_block,
            value_block,
            score_scale,
        )
        begin = block_index * step_rows
        key_buffer = lax.dynamic_update_slice_in_dim(
            key_buffer, grad_key.reshape(step_rows, head_count * HD), begin, 0
        )
        value_buffer = lax.dynamic_update_slice_in_dim(
            value_buffer, grad_value.reshape(step_rows, head_count * HD), begin, 0
        )
        return (query_acc + add_query, key_buffer, value_buffer)

    empty_grads = jnp.zeros((span_rows, head_count * HD), jnp.float32)
    self_dq, key_terms, value_terms = lax.fori_loop(
        0, all_blocks, backward_step, (query_zero, empty_grads, empty_grads)
    )
    grad_self_key, grad_self_value = (
        lax.psum_scatter(
            key_terms.astype(jnp.bfloat16), "dec", scatter_dimension=0, tiled=True
        ).astype(jnp.float32),
        lax.psum_scatter(
            value_terms.astype(jnp.bfloat16), "dec", scatter_dimension=0, tiled=True
        ).astype(jnp.float32),
    )
    self_out = self_context.transpose(1, 0, 2).reshape(tok_rows, head_count * HD)
    grad_self_query = self_dq.transpose(1, 0, 2).reshape(tok_rows, head_count * HD)
    cross_query = jnp.dot(tokens, w_query, preferred_element_type=jnp.float32).astype(jnp.bfloat16)
    cross_heads = cross_query.reshape(tok_rows, head_count, HD)
    cross_grads = grad_cross.reshape(tok_rows, head_count, HD)

    def project_keys(shard_piece):
        piece_rows = shard_piece.shape[0]
        key_block = (
            jnp.dot(shard_piece, w_key, preferred_element_type=jnp.float32)
            .astype(jnp.bfloat16)
            .reshape(piece_rows, head_count, HD)
        )
        value_block = (
            jnp.dot(shard_piece, w_value, preferred_element_type=jnp.float32)
            .astype(jnp.bfloat16)
            .reshape(piece_rows, head_count, HD)
        )
        scores = (
            jnp.einsum("rhd,khd->hrk", cross_heads, key_block, preferred_element_type=jnp.float32)
            * score_scale
        )
        return (scores, key_block, value_block)

    scores, key_block, value_block = project_keys(
        lax.all_gather(context, "enc", axis=0, tiled=True)
    )
    cross_max, cross_norm, cross_sum = online_update(initial, scores, value_block)
    cross_context = (cross_sum / cross_norm).astype(jnp.bfloat16)
    cross_log = cross_max + jnp.log(cross_norm)
    cross_delta = jnp.sum(
        cross_grads.astype(jnp.float32).transpose(1, 0, 2) * cross_context.astype(jnp.float32),
        axis=2,
        keepdims=True,
    )
    shard_piece = lax.all_gather(context, "enc", axis=0, tiled=True)
    query_acc = query_zero
    scores, key_block, value_block = project_keys(shard_piece)
    add_query, grad_key, grad_value = backward_terms(
        scores,
        cross_log,
        cross_delta,
        cross_heads,
        cross_grads,
        key_block,
        value_block,
        score_scale,
    )
    piece_rows = shard_piece.shape[0]
    key_low = grad_key.reshape(piece_rows, head_count * HD).astype(jnp.bfloat16)
    value_low = grad_value.reshape(piece_rows, head_count * HD).astype(jnp.bfloat16)
    key_weight = jnp.einsum("kc,ke->ce", shard_piece, key_low, preferred_element_type=jnp.float32)
    value_weight = jnp.einsum(
        "kc,ke->ce", shard_piece, value_low, preferred_element_type=jnp.float32
    )
    cross_dq, key_weight, value_weight = (add_query, key_weight, value_weight)
    query_low = cross_dq.transpose(1, 0, 2).reshape(tok_rows, head_count * HD).astype(jnp.bfloat16)
    query_weight = jnp.einsum("rc,re->ce", tokens, query_low, preferred_element_type=jnp.float32)
    grad_w_query, grad_w_key, grad_w_value = (
        lax.psum_scatter(
            query_weight.astype(jnp.bfloat16), "dec", scatter_dimension=0, tiled=True
        ).astype(jnp.float32),
        lax.psum_scatter(
            key_weight.astype(jnp.bfloat16), "dec", scatter_dimension=0, tiled=True
        ).astype(jnp.float32),
        lax.psum_scatter(
            value_weight.astype(jnp.bfloat16), "dec", scatter_dimension=0, tiled=True
        ).astype(jnp.float32),
    )
    cross_out = cross_context.transpose(1, 0, 2).reshape(tok_rows, head_count * HD)
    return (
        self_out,
        grad_self_query,
        grad_self_key,
        grad_self_value,
        cross_out,
        grad_w_query,
        grad_w_key,
        grad_w_value,
    )


def solution(mesh):
    placed = (
        P("dec", None),
        P(None, "enc"),
        P("enc", None),
        P(None, "enc"),
        P(None, "enc"),
        P("dec", "enc"),
        P("dec", "enc"),
        P("dec", "enc"),
        P("dec", "enc"),
        P("dec", "enc"),
    )
    return jax.shard_map(
        body,
        mesh=mesh,
        in_specs=placed,
        out_specs=(
            P("dec", "enc"),
            P("dec", "enc"),
            P("dec", "enc"),
            P("dec", "enc"),
            P("dec", "enc"),
            P("dec", "enc"),
            P("dec", "enc"),
            P("dec", "enc"),
        ),
        check_vma=False,
    )
```

profile of v0, /device:TPU:0, one launch (start us, length us, event | category | flops | bytes accessed | tf_op | source)
XLA Modules:
  0.0 547.6 jit_solution(15466335458142395612)
XLA Ops:
  14.4 44.3 %all-gather.4.cloned.1.call-done = bf16[2048,256]{0,1:T(8,128)(2,1)} async-done(((bf16[256,256]{0,1:T(8,128)(2,1)}), bf16[2048,256]{0,1:T(8,128)(2,1)}) %all-gather.4.cloned.1.call-update) | async-done | bytes 1048592 | tf_op jit(solution)/shard_map/all_gather | solution.py:74
  58.7 46.4 %all-gather.6.cloned.1.call-done = bf16[2048,256]{0,1:T(8,128)(2,1)} async-done(((bf16[256,256]{0,1:T(8,128)(2,1)}), bf16[2048,256]{0,1:T(8,128)(2,1)}) %all-gather.6.cloned.1.call-update) | async-done | bytes 1048592 | tf_op jit(solution)/shard_map/all_gather | solution.py:75
  105.1 18.2 %while.36 = (s32[]{:T(128)}, f32[2,256,1]{1,0,2:T(2,128)S(1)}, f32[2,256,1]{1,0,2:T(2,128)S(1)}, f32[2,256,128]{2,1,0:T(8,128)}, bf16[2048,256]{0,1:T(8,128)(2,1...) while((s32[]{:T(128)}, f32[2,256,1]{1,0,2:T(2,128)S(1)}, ...), condition=%wide.region_3.4_spmd.clone, body=%wide.region_0.3_spmd.clone.sunk | while | flops 136384000 | bytes 5674167 | solution.py:108
  121.1 2.0 convolution_add_fusion.4
  127.3 41.9 %while.37 = (s32[]{:T(128)}, f32[2,256,128]{2,1,0:T(8,128)}, bf16[2048,256]{1,0:T(8,128)(2,1)}, bf16[2048,256]{1,0:T(8,128)(2,1)}, bf16[2048,256]{0,1:T(8,128)(2...) while((s32[]{:T(128)}, f32[2,256,128]{2,1,0:T(8,128)}, ...), condition=%wide.region_6.7_spmd.clone, body=%wide.region_5.6_spmd.clone.sunk | while | flops 337904128 | bytes 15213837 | solution.py:141
  131.8 2.2 fusion.118
  141.6 2.2 fusion.118
  152.3 2.2 fusion.118
  163.0 2.2 fusion.118
  170.3 2.5 convolution_convert_fusion.8
  173.1 5.8 %convolution_convert_fusion.1 = bf16[4096,256]{0,1:T(8,128)(2,1)S(1)} fusion(bf16[4096,1024]{1,0:T(8,128)(2,1)} %all-gather.8.cloned.1.call-done, bf16[1024,256]{1,0:T(8,128)(2,1)S(1)} %copy-done.9), kind=kOutput, calls=%fused_computation.50 | convolution fusion | flops 2148532224 | bytes 11010048 | tf_op jit(solution)/shard_map/dot_general | solution.py:161
  181.8 7.5 %convolution_convert_fusion = bf16[4096,256]{0,1:T(8,128)(2,1)S(1)} fusion(bf16[4096,1024]{1,0:T(8,128)(2,1)} %all-gather.8.cloned.1.call-done, bf16[1024,256]{1,0:T(8,128)(2,1)S(1)} %copy-done.10), kind=kOutput, calls=%fused_computation.49 | convolution fusion | flops 2148532224 | bytes 11010048 | tf_op jit(solution)/shard_map/dot_general | solution.py:166
  189.3 2.1 fusion.36
  191.5 2.6 fusion.22
  196.7 5.8 %fusion.32 = bf16[1024,256]{0,1:T(8,128)(2,1)S(1)} fusion(bf16[4096,256]{0,1:T(8,128)(2,1)S(1)} %bitcast.203, bf16[4096,1024]{1,0:T(8,128)(2,1)} %all-gather.8.cloned.1.call-done), kind=kOutput, calls=%fused_computation.60 | convolution fusion | flops 2147745792 | bytes 11010048 | tf_op jit(solution)/shard_map/kc,ke->ce/dot_general | solution.py:203
  203.6 5.0 convolution_convert_fusion.2
  208.6 5.8 %fusion.33 = bf16[1024,256]{0,1:T(8,128)(2,1)S(1)} fusion(bf16[4096,256]{0,1:T(8,128)(2,1)S(1)} %bitcast.202, bf16[4096,1024]{1,0:T(8,128)(2,1)} %all-gather.8.cloned.1.call-done), kind=kOutput, calls=%fused_computation.61 | convolution fusion | flops 2147745792 | bytes 11010048 | tf_op jit(solution)/shard_map/kc,ke->ce/dot_general | solution.py:204
  215.5 4.4 convolution_convert_fusion.7
  220.0 2.1 fusion.26
  223.6 15.8 %reduce-scatter.10.cloned.1.call-done = bf16[256,256]{1,0:T(8,128)(2,1)} async-done(((bf16[2048,256]{1,0:T(8,128)(2,1)}), bf16[256,256]{1,0:T(8,128)(2,1)}) %reduce-scatter.10.cloned.1.call-update) | async-done | bytes 131088 | tf_op jit(solution)/shard_map/reduce_scatter | solution.py:145
  241.0 73.1 %reduce-scatter.12.cloned.1.call-done = bf16[256,256]{1,0:T(8,128)(2,1)} async-done(((bf16[2048,256]{1,0:T(8,128)(2,1)}), bf16[256,256]{1,0:T(8,128)(2,1)}) %reduce-scatter.12.cloned.1.call-update) | async-done | bytes 131088 | tf_op jit(solution)/shard_map/reduce_scatter | solution.py:148
  316.5 71.1 %reduce-scatter.16.cloned.1.call-done = bf16[128,256]{1,0:T(8,128)(2,1)} async-done(((bf16[1024,256]{1,0:T(8,128)(2,1)}), bf16[128,256]{1,0:T(8,128)(2,1)}) %reduce-scatter.16.cloned.1.call-update) | async-done | bytes 65552
  389.3 71.8 %reduce-scatter.18.cloned.1.call-done = bf16[128,256]{1,0:T(8,128)(2,1)} async-done(((bf16[1024,256]{1,0:T(8,128)(2,1)}), bf16[128,256]{1,0:T(8,128)(2,1)}) %reduce-scatter.18.cloned.1.call-update) | async-done | bytes 65552
  462.8 76.1 %reduce-scatter.14.cloned.1.call-done = bf16[512,256]{0,1:T(8,128)(2,1)} async-done(((bf16[4096,256]{0,1:T(8,128)(2,1)}), bf16[512,256]{0,1:T(8,128)(2,1)}) %reduce-scatter.14.cloned.1.call-update) | async-done | bytes 262160 | tf_op jit(solution)/shard_map/reduce_scatter | solution.py:211
  (165 shorter events, 79.6 us)
Async XLA Ops:
  7.2 163.1 %copy-start = (bf16[256,4096]{1,0:T(8,128)(2,1)S(1)}, bf16[256,4096]{1,0:T(8,128)(2,1)}, u32[]{:S(2)}) copy-start(bf16[256,4096]{1,0:T(8,128)(2,1)} %param.14) | copy-start | bytes 6291460
  7.2 51.5 %all-gather.4.cloned.1.call-start = ((), (), s32[]{:S(2)}) async-start(), calls=%async_computation.5 | async-start | bytes 1179648 | tf_op jit(solution)/shard_map/all_gather | solution.py:74
  9.1 96.0 %all-gather.6.cloned.1.call-start = ((), (), s32[]{:S(2)}) async-start(), calls=%async_computation.6 | async-start | bytes 1179648 | tf_op jit(solution)/shard_map/all_gather | solution.py:75
  10.8 162.3 %all-gather.8.cloned.1.call-start = ((), (), s32[]{:S(2)}) async-start(), calls=%async_computation.9 | async-start | bytes 8912896 | tf_op jit(solution)/shard_map/all_gather | solution.py:177
  11.5 227.8 %reduce-scatter.10.cloned.1.call-start = ((), (), s32[]{:S(2)}) async-start(), calls=%async_computation.7 | async-start | bytes 1179648 | tf_op jit(solution)/shard_map/reduce_scatter | solution.py:145
  12.6 92.5 %copy-start.6 = (bf16[256,256]{0,1:T(8,128)(2,1)}, bf16[256,256]{0,1:T(8,128)(2,1)S(1)}, u32[]{:S(2)}) copy-start(bf16[256,256]{0,1:T(8,128)(2,1)S(1)} %copy.85) | copy-start | bytes 393220
  127.3 4.1 copy-start.7
  129.8 1.2 copy-start.2
  137.0 4.1 copy-start.7
  139.5 1.2 copy-start.2
  147.7 4.1 copy-start.7
  158.4 4.1 copy-start.7
  161.0 1.2 copy-start.2
  169.2 4.0 copy-start.9
  169.2 144.9 %reduce-scatter.12.cloned.1.call-start = ((), (), s32[]{:S(2)}) async-start(), calls=%async_computation.8 | async-start | bytes 1179648 | tf_op jit(solution)/shard_map/reduce_scatter | solution.py:148
  172.8 214.7 %reduce-scatter.16.cloned.1.call-start = ((), (), s32[]{:S(2)}) async-start(), calls=%async_computation.11 | async-start | bytes 589824
  178.9 1.5 copy-start.5
  180.4 11.1 %copy-start.1 = (f32[2,256,4096]{2,1,0:T(8,128)}, f32[2,256,4096]{2,1,0:T(8,128)S(1)}, u32[]{:S(2)}) copy-start(f32[2,256,4096]{2,1,0:T(8,128)S(1)} %get-tuple-element.511) | copy-start | bytes 25165828
  180.4 1.4 copy-start.10
  194.0 1.9 copy-start.3
  203.6 257.5 %reduce-scatter.18.cloned.1.call-start = ((), (), s32[]{:S(2)}) async-start(), calls=%async_computation.12 | async-start | bytes 589824
  215.5 323.4 %reduce-scatter.14.cloned.1.call-start = ((), (), s32[]{:S(2)}) async-start(), calls=%async_computation.10 | async-start | bytes 2359296 | tf_op jit(solution)/shard_map/reduce_scatter | solution.py:211
  220.0 2.1 copy-start.8
  220.0 2.9 copy-start.4
  (1 other events, 1.2 us)
Sparse Core Ops, SparseCore 0:
  10.8 47.8 all-gather.3
  61.5 43.5 all-gather.5
  106.8 50.2 all-gather.7
  169.3 70.0 reduce-scatter.9
  243.2 70.8 reduce-scatter.11
  318.1 69.4 reduce-scatter.15
  391.5 69.5 reduce-scatter.17
  464.8 74.0 reduce-scatter.13
where the time goes:
time: 549 us; the launch traced here: 548 us
  waiting for transfers between devices  399 us (73%)
  matrix products  81.9 us (15%)
  local copies, waits for them, and re-layouts  43.6 us (8%)
  between operations  14.4 us (3%)
  other arithmetic  7.25 us (1%)
    unnamed x10, waiting for transfers between devices  144 us
    reduce_scatter x1, waiting for transfers between devices, body(): lax.psum_scatter(query_weight.astype(jnp.bfloat16), 'dec', scatter_dimens...  76.1 us
    reduce_scatter x1, waiting for transfers between devices, body(): lax.psum_scatter(value_terms.astype(jnp.bfloat16), 'dec', scatter_dimensi...  73.1 us
    all_gather x1, waiting for transfers between devices, body(): lax.all_gather(self_value, 'dec', axis=0, tiled=True)  46.4 us
    all_gather x1, waiting for transfers between devices, body(): lax.all_gather(self_key, 'dec', axis=0, tiled=True)  44.3 us
    unnamed x32, local copies, waits for them, and re-layouts  17.5 us
    reduce_scatter x1, waiting for transfers between devices, body(): lax.psum_scatter(key_terms.astype(jnp.bfloat16), 'dec', scatter_dimension...  15.8 us
    dot_general x5, matrix products, backward_terms(): jnp.einsum('hrk,rhd->khd', probability.astype(jnp.bfloat16), grad_heads,...  13.9 us
  transfers between devices with their start and end apart: 8, of which 7 were waited for; matrix products, arithmetic and copies ran while one was open for 23% of the time, Pallas kernels for 0%

commit v1 on v0

v1 whole, which is shorter than its diff:
```python
import jax
import jax.numpy as jnp
from jax import lax
from jax.experimental import pallas as pl
from jax.experimental.pallas import tpu as pltpu
from jax.sharding import PartitionSpec as P

MESH = pl.DeviceIdType.MESH
HD = 128
SCALE = HD ** -0.5
ROWS = 256
F32 = jnp.float32
BF16 = jnp.bfloat16


def nn(a, b):
    return jnp.dot(a, b, preferred_element_type=F32)


def nt(a, b):
    return lax.dot_general(a, b, (((1,), (1,)), ((), ())), preferred_element_type=F32)


def kernel(
    tok_h, wq_h, ctx_h, wk_h, wv_h, sq_h, sk_h, sv_h, gs_h, gc_h,
    o_self, o_dsq, o_dsk, o_dsv, o_cross, o_gwq, o_gwk, o_gwv,
    tok, wq, wkv, wkvt, own, gc, ctx, kvt, wst, dpst, mst, dkvt,
    cm, cl, cacc, sm, sl, sacc, blk, stat, tb, dqt, wsend, wrecv,
    lsem, ssem, ctx_sem, sib_sem, blk_sem, stat_sem, tok_sem, tokg_sem, tsib_sem, dq_sem, w_sem,
):
    e = lax.axis_index("enc")
    d = lax.axis_index("dec")
    y, low = e // 4, e % 4
    core = e % 2
    yup = lax.rem(y + 1, 4) * 4 + low
    ydn = lax.rem(y + 3, 4) * 4 + low
    yfar = lax.rem(y + 2, 4) * 4 + low
    sib = e + 1 - 2 * core
    xflip = e + 2 - 4 * ((e // 2) % 2)
    xh = d // 4

    def peer(m):
        out = d
        for bit in (1, 2, 4):
            if m & bit:
                out = out + bit - 2 * bit * ((d // bit) % 2)
        return out

    dev = {
        "yup": (yup, d), "ydn": (ydn, d), "yfar": (yfar, d), "sib": (sib, d),
        "xi": (xflip, d), "xo": (xflip, peer(4)),
    }
    partner = [(e, peer(m)) for m in range(8)]

    barrier = pltpu.get_barrier_semaphore()
    greet = list(dev.values()) + partner[1:]
    for target in greet:
        pl.semaphore_signal(barrier, inc=1, device_id=target, device_id_type=MESH)

    loads = []

    def load(src, dst):
        copy = pltpu.make_async_copy(src, dst, lsem.at[len(loads)])
        copy.start()
        loads.append(copy)
        return copy

    l_own = [load(r, own.at[i]) for i, r in enumerate((sk_h, sv_h, sq_h, gs_h))]
    l_ctx = load(ctx_h, ctx.at[0, 0])
    l_wk = load(wk_h, wkv.at[:, pl.ds(0, ROWS)])
    l_wv = load(wv_h, wkv.at[:, pl.ds(ROWS, ROWS)])
    l_gc = load(gc_h, gc)
    l_tok = load(tok_h, tok)
    l_wq = load(wq_h, wq)

    sends = []

    def send(src, dst, rsem, target):
        copy = pltpu.make_async_remote_copy(
            src_ref=src, dst_ref=dst, send_sem=ssem.at[len(sends)], recv_sem=rsem,
            device_id=target, device_id_type=MESH,
        )
        copy.start()
        sends.append(copy)

    def arrived(dst, rsem):
        pltpu.make_async_remote_copy(
            src_ref=dst, dst_ref=dst, send_sem=ssem.at[0], recv_sem=rsem,
            device_id=dev["sib"], device_id_type=MESH,
        ).wait_recv()

    half = ROWS // 2

    def part(k, h, side=0):
        return ctx.at[k, side, pl.ds(h * half, half), :]

    def whole_out(k, h, src, target):
        send(src, part(k, h), ctx_sem.at[k, h], target)

    def got(k, h):
        arrived(part(k, h), ctx_sem.at[k, h])

    def share(k, h):
        send(part(k, h), part(k, h, 1), sib_sem.at[k, h], dev["sib"])

    def shared(k):
        for h in range(2):
            arrived(part(k, h, 1), sib_sem.at[k, h])

    for c in l_own:
        c.wait()
    l_ctx.wait()
    pl.semaphore_wait(barrier, len(greet))

    whole_out(6, 0, part(0, 0), dev["yup"])
    whole_out(2, 1, part(0, 1), dev["ydn"])
    whole_out(1, 0, part(0, 0), dev["xi"])
    whole_out(1, 1, part(0, 1), dev["xo"])
    share(0, 0)
    share(0, 1)
    whole_out(6, 1, part(0, 1), dev["yup"])
    whole_out(2, 0, part(0, 0), dev["ydn"])

    def own_block(m):
        first = 2 * (1 - ((d // (1 if m == 1 else 2 if m < 4 else 4)) % 2))
        return own.at[pl.ds(2 - first, 2)]

    def blk_out(m, slot, src):
        send(src, blk.at[slot], blk_sem.at[slot], partner[m])

    blk_out(4, 4, own_block(4))
    blk_out(1, 1, own_block(1))
    blk_out(3, 3, own_block(3))
    blk_out(2, 2, own_block(2))

    l_wk.wait()
    l_wv.wait()
    wkvt[...] = wkv[...].T
    l_tok.wait()
    l_wq.wait()
    cq32 = nn(tok[...], wq[...])
    cq = cq32.astype(BF16)
    cqt = cq.T
    l_gc.wait()
    gcv = gc[...]
    gct = gcv.T

    def hs(h):
        return slice(h * HD, (h + 1) * HD)

    def cross_forward(k, first):
        x = ctx[k].reshape(2 * ROWS, ctx.shape[3])
        kv = nt(wkvt[...], x).astype(BF16)
        cols = slice(k * 2 * ROWS, (k + 1) * 2 * ROWS)
        kvt[:, cols] = kv
        for h in range(2):
            s = nn(cq[:, hs(h)], kv[hs(h)]) * SCALE
            top = jnp.max(s, axis=1, keepdims=True)
            if not first:
                old = cm[h]
                top = jnp.maximum(old, top)
            w = jnp.exp(s - top)
            wst[h, :, cols] = w
            dpst[h, :, cols] = nn(gcv[:, hs(h)], kv[hs(2 + h)])
            add_l = jnp.sum(w, axis=1, keepdims=True)
            add_o = nt(w.astype(BF16), kv[hs(2 + h)])
            if not first:
                fix = jnp.exp(old - top)
                add_l = add_l + cl[h] * fix
                add_o = add_o + cacc[h] * fix
            cm[h] = top
            cl[h] = add_l
            cacc[h] = add_o
            mst[k, h] = top

    shared(0)
    cross_forward(0, True)

    got(6, 0)
    whole_out(4, 0, part(6, 0), dev["yup"])
    whole_out(7, 0, part(6, 0), dev["xi"])
    share(6, 0)
    got(2, 1)
    whole_out(4, 1, part(2, 1), dev["ydn"])
    whole_out(3, 1, part(2, 1), dev["xo"])
    share(2, 1)
    for h in range(2):
        got(1, h)
        share(1, h)
    got(6, 1)
    whole_out(7, 1, part(6, 1), dev["xo"])
    share(6, 1)
    got(2, 0)
    whole_out(3, 0, part(2, 0), dev["xi"])
    share(2, 0)
    arrived(blk.at[4], blk_sem.at[4])
    for m in (1, 3, 2):
        blk_out(m, 4 + m, blk.at[4])
    lane = (y * 2 + core) * 32
    trows = pl.ds(pl.multiple_of(lane, 32), 32)

    def tcols(p):
        return pl.ds(pl.multiple_of(p * 512, 512), 512)

    for m in range(1, 8):
        send(tok.at[trows, tcols(partner[m][1])], tb.at[m, trows], tok_sem.at[m], partner[m])
    l_tb = load(tok.at[:, tcols(d)], tb.at[0])

    shared(1)
    cross_forward(1, False)
    shared(6)
    cross_forward(6, False)
    shared(2)
    cross_forward(2, False)

    got(7, 0)
    whole_out(5, 0, part(7, 0), dev["yup"])
    share(7, 0)
    got(3, 1)
    whole_out(5, 1, part(3, 1), dev["ydn"])
    share(3, 1)
    got(4, 0)
    share(4, 0)
    got(4, 1)
    share(4, 1)
    got(7, 1)
    share(7, 1)
    got(3, 0)
    share(3, 0)
    shared(4)
    cross_forward(4, False)
    shared(7)
    cross_forward(7, False)
    shared(3)
    cross_forward(3, False)
    for m in range(1, 8):
        arrived(tb.at[m, trows], tok_sem.at[m])
    l_tb.wait()

    def trange(ee):
        return pl.ds(pl.multiple_of((ee // 4 * 2 + ee % 2) * 32, 32), 32)

    moved = tb.at[pl.ds(1, 7), trows]
    for i, name in enumerate(("yup", "ydn", "yfar", "sib")):
        send(moved, moved, tokg_sem.at[i], dev[name])
    got(5, 0)
    share(5, 0)
    got(5, 1)
    share(5, 1)
    shared(5)
    cross_forward(5, False)

    for h in range(2):
        norm = cl[h]
        out = (cacc[h] / norm).astype(BF16)
        o_cross[:, hs(h)] = out
        g = gcv[:, hs(h)]
        lse = cm[h] + jnp.log(norm)
        delta = jnp.sum(g.astype(F32) * out.astype(F32), axis=1, keepdims=True)
        qt = cqt[hs(h)]
        gt = gct[hs(h)]
        dq = None
        for k in range(8):
            cols = slice(k * 2 * ROWS, (k + 1) * 2 * ROWS)
            p = wst[h, :, cols] * jnp.exp(mst[k, h] - lse)
            ds = (p * (dpst[h, :, cols] - delta) * SCALE).astype(BF16)
            add = nt(ds, kvt[hs(h), cols])
            dq = add if dq is None else dq + add
            dkvt[hs(h), cols] = nn(qt, ds).astype(BF16)
            dkvt[hs(2 + h), cols] = nn(gt, p.astype(BF16)).astype(BF16)
        dqt[0, hs(h), :] = dq.astype(BF16).T
    for m in (4, 5, 6, 7, 2, 1, 3):
        send(dqt.at[0], dqt.at[m], dq_sem.at[m], partner[m])

    odd = d % 2
    ctx2 = ctx.reshape(16 * ROWS, ctx.shape[3])
    for j in (2, 3, 1, 0):
        lo = partner[2 * j][1] // 2 * 256
        piece = nn(dkvt[...], ctx2[:, pl.ds(pl.multiple_of(lo, 256), 256)]).astype(BF16)
        for b in range(2):
            wsend[j, b] = piece[:, b * 128:(b + 1) * 128]
        for r in range(2):
            m = 2 * j + r
            if m:
                src = wsend.at[j, odd if r == 0 else 1 - odd]
                send(src, wrecv.at[m], w_sem.at[m], partner[m])

    row = lax.broadcasted_iota(jnp.int32, (ROWS, ROWS), 0)
    col = lax.broadcasted_iota(jnp.int32, (ROWS, ROWS), 1)

    def xor_slot(p):
        a, b = d, p
        out = 0
        for bit in (1, 2, 4):
            out = out + bit * (((a // bit) + (b // bit)) % 2)
        return out

    for h in range(2):
        s = jnp.where(row >= col, nt(own[2, :, hs(h)], own[0, :, hs(h)]) * SCALE, -1e30)
        top = jnp.max(s, axis=1, keepdims=True)
        w = jnp.exp(s - top)
        sm[h] = top
        sl[h] = jnp.sum(w, axis=1, keepdims=True)
        sacc[h] = nn(w.astype(BF16), own[1, :, hs(h)])

    for m in (1, 2, 3, 5, 6, 7):
        arrived(blk.at[m], blk_sem.at[m])

    def self_forward(p, carry):
        slot = xor_slot(p)
        for h in range(2):
            s = nt(own[2, :, hs(h)], blk[slot, 0, :, hs(h)]) * SCALE
            old = sm[h]
            top = jnp.maximum(old, jnp.max(s, axis=1, keepdims=True))
            w = jnp.exp(s - top)
            fix = jnp.exp(old - top)
            sm[h] = top
            sl[h] = sl[h] * fix + jnp.sum(w, axis=1, keepdims=True)
            sacc[h] = sacc[h] * fix + nn(w.astype(BF16), blk[slot, 1, :, hs(h)])
        return carry

    lax.fori_loop(0, d, self_forward, 0)
    for h in range(2):
        norm = sl[h]
        out = (sacc[h] / norm).astype(BF16)
        o_self[:, hs(h)] = out
        g = own[3, :, hs(h)]
        lse = sm[h] + jnp.log(norm)
        delta = jnp.sum(g.astype(F32) * out.astype(F32), axis=1, keepdims=True)
        sm[h] = lse
        sl[h] = delta
        stat[0, 2 * h:2 * h + 1, :] = jnp.broadcast_to(lse, (ROWS, HD)).T[0:1]
        stat[0, 2 * h + 1:2 * h + 2, :] = jnp.broadcast_to(delta, (ROWS, HD)).T[0:1]
    for m in range(1, 8):
        send(stat.at[0], stat.at[m], stat_sem.at[m], partner[m])

    def query_grad(h, s, v, k):
        p = jnp.exp(s - sm[h])
        dp = nt(own[3, :, hs(h)], v)
        return nn((p * (dp - sl[h]) * SCALE).astype(BF16), k)

    for h in range(2):
        k = own[0, :, hs(h)]
        s = jnp.where(row >= col, nt(own[2, :, hs(h)], k) * SCALE, -1e30)
        o_dsq[:, hs(h)] = query_grad(h, s, own[1, :, hs(h)], k)

    def self_query(p, carry):
        slot = xor_slot(p)
        for h in range(2):
            k = blk[slot, 0, :, hs(h)]
            s = nt(own[2, :, hs(h)], k) * SCALE
            o_dsq[:, hs(h)] += query_grad(h, s, blk[slot, 1, :, hs(h)], k)
        return carry

    lax.fori_loop(0, d, self_query, 0)

    def key_grad(h, st, q, g, lse, delta):
        p = jnp.exp(st - lse)
        dp = nt(own[1, :, hs(h)], g)
        ds = (p * (dp - delta) * SCALE).astype(BF16)
        return nn(ds, q), nn(p.astype(BF16), g)

    for h in range(2):
        q, g = own[2, :, hs(h)], own[3, :, hs(h)]
        st = jnp.where(col >= row, nt(own[0, :, hs(h)], q) * SCALE, -1e30)
        dk, dv = key_grad(h, st, q, g, stat[0, 2 * h:2 * h + 1], stat[0, 2 * h + 1:2 * h + 2])
        o_dsk[:, hs(h)] = dk
        o_dsv[:, hs(h)] = dv
    for m in range(1, 8):
        arrived(stat.at[m], stat_sem.at[m])

    def self_key(p, carry):
        slot = xor_slot(p)
        for h in range(2):
            q, g = blk[slot, 0, :, hs(h)], blk[slot, 1, :, hs(h)]
            st = nt(own[0, :, hs(h)], q) * SCALE
            dk, dv = key_grad(
                h, st, q, g, stat[slot, 2 * h:2 * h + 1], stat[slot, 2 * h + 1:2 * h + 2]
            )
            o_dsk[:, hs(h)] += dk
            o_dsv[:, hs(h)] += dv
        return carry

    lax.fori_loop(d + 1, 8, self_key, 0)

    for i, ee in enumerate((ydn, yup, yfar, sib)):
        spot = tb.at[pl.ds(1, 7), trange(ee)]
        arrived(spot, tokg_sem.at[i])
    others = []
    for i, ee in enumerate((ydn, yup, yfar)):
        spot = tb.at[pl.ds(1, 7), trange(ee)]
        send(spot, spot, tsib_sem.at[i], dev["sib"])
    for i, ee in enumerate((ydn, yup, yfar)):
        ss = ee + 1 - 2 * core
        arrived(tb.at[pl.ds(1, 7), trange(ss)], tsib_sem.at[i])
    gw = None
    for m in range(8):
        if m:
            arrived(dqt.at[m], dq_sem.at[m])
        add = nn(dqt[m], tb[m])
        gw = add if gw is None else gw + add
    o_gwq[...] = gw.T

    total = wsend[0, odd].astype(F32)
    for m in range(1, 8):
        arrived(wrecv.at[m], w_sem.at[m])
        total = total + wrecv[m].astype(F32)
    o_gwk[...] = total[0:256].T
    o_gwv[...] = total[256:512].T

    for copy in sends:
        copy.wait_send()


def body(*args):
    vm, any_ = pl.BlockSpec(memory_space=pltpu.VMEM), pl.BlockSpec(memory_space=pl.ANY)
    shape = jax.ShapeDtypeStruct
    block = (ROWS, ROWS)
    dma = pltpu.SemaphoreType.DMA
    return tuple(pl.pallas_call(
        kernel,
        out_shape=(
            shape(block, BF16), shape(block, F32), shape(block, F32), shape(block, F32),
            shape(block, BF16), shape((512, ROWS), F32), shape((128, ROWS), F32),
            shape((128, ROWS), F32),
        ),
        in_specs=[any_] * 10,
        out_specs=[vm] * 8,
        scratch_shapes=[
            pltpu.VMEM((256, 4096), BF16),
            pltpu.VMEM((4096, 256), BF16),
            pltpu.VMEM((1024, 512), BF16),
            pltpu.VMEM((512, 1024), BF16),
            pltpu.VMEM((4, 256, 256), BF16),
            pltpu.VMEM((256, 256), BF16),
            pltpu.VMEM((8, 2, 256, 1024), BF16),
            pltpu.VMEM((512, 4096), BF16),
            pltpu.VMEM((2, 256, 4096), F32),
            pltpu.VMEM((2, 256, 4096), F32),
            pltpu.VMEM((8, 2, 256, 1), F32),
            pltpu.VMEM((512, 4096), BF16),
            pltpu.VMEM((2, 256, 1), F32),
            pltpu.VMEM((2, 256, 1), F32),
            pltpu.VMEM((2, 256, 128), F32),
            pltpu.VMEM((2, 256, 1), F32),
            pltpu.VMEM((2, 256, 1), F32),
            pltpu.VMEM((2, 256, 128), F32),
            pltpu.VMEM((8, 2, 256, 256), BF16),
            pltpu.VMEM((8, 8, 256), F32),
            pltpu.VMEM((8, 256, 512), BF16),
            pltpu.VMEM((8, 256, 256), BF16),
            pltpu.VMEM((4, 2, 512, 128), BF16),
            pltpu.VMEM((8, 512, 128), BF16),
            dma((16,)), dma((80,)), dma((8, 2)), dma((8, 2)), dma((8,)), dma((8,)), dma((8,)),
            dma((4,)), dma((3,)), dma((8,)), dma((8,)),
        ],
        compiler_params=pltpu.CompilerParams(
            collective_id=0, has_side_effects=True, vmem_limit_bytes=62 << 20
        ),
        name="layer",
    )(*args))


def solution(mesh):
    placed = (
        P("dec", None), P(None, "enc"), P("enc", None), P(None, "enc"), P(None, "enc"),
    ) + (P("dec", "enc"),) * 5
    return jax.shard_map(
        body, mesh=mesh, in_specs=placed, out_specs=(P("dec", "enc"),) * 8, check_vma=False
    )
```

time: 549 us -> 95.7 us (0.17)
  the two profiles are of different devices: /device:TPU:0 before, /device:TPU:25 now
where the time goes in v1:
time: 95.7 us; the launch traced here: 95.4 us
  Pallas kernels  84.4 us (88%)
  local copies, waits for them, and re-layouts  10.3 us (11%)
    pallas_call x1, Pallas kernels, body(): pl.pallas_call(kernel, out_shape=(shape(block, BF16), shape(block, F32),...  84.4 us
    unnamed x14, local copies, waits for them, and re-layouts  10.3 us

profile of v1, /device:TPU:25, one launch (start us, length us, event | category | flops | bytes accessed | tf_op | source)
XLA Modules:
  0.0 95.4 jit_solution(1278051460779570691)
XLA Ops:
  0.6 84.4 %layer.1 = (bf16[256,256]{1,0:T(8,128)(2,1)}, f32[256,256]{1,0:T(8,128)}, f32[256,256]{1,0:T(8,128)}, f32[256,256]{1,0:T(8,128)}, bf16[256,256]{1,0:T(8,128)(2,1...) custom-call(bf16[256,4096]{1,0:T(8,128)(2,1)} %tok_h.1, bf16[4096,256]{1,0:T(8,128)(2,1)} %wq_h.1, ...), custom_call_target="tpu_custom_call" | custom-call | tf_op jit(solution)/shard_map/layer/pallas_call | solution.py:420
  85.1 0.0 copy-start
  85.1 0.0 copy-start.2
  85.1 0.0 copy-start.1
  85.1 1.6 %copy.26 = bf16[256,256]{1,0:T(8,128)(2,1)} copy(bf16[256,256]{1,0:T(8,128)(2,1)} %get-tuple-element.16) | data formatting | bytes 262144
  86.8 1.7 %copy.27 = f32[256,256]{1,0:T(8,128)} copy(f32[256,256]{1,0:T(8,128)} %get-tuple-element.17) | data formatting | bytes 524288
  88.4 1.7 %copy.28 = f32[256,256]{1,0:T(8,128)} copy(f32[256,256]{1,0:T(8,128)} %get-tuple-element.18) | data formatting | bytes 524288
  90.1 1.7 %copy.29 = f32[256,256]{1,0:T(8,128)} copy(f32[256,256]{1,0:T(8,128)} %get-tuple-element.19) | data formatting | bytes 524288
  91.8 1.6 %copy.30 = bf16[256,256]{1,0:T(8,128)(2,1)} copy(bf16[256,256]{1,0:T(8,128)(2,1)} %get-tuple-element.20) | data formatting | bytes 262144
  93.3 0.0 copy-done
  93.3 0.8 copy.31
  94.1 0.0 copy-done.2
  94.1 0.7 copy.32
  94.8 0.0 copy-done.1
  94.8 0.7 copy.33
Async XLA Ops:
  85.1 8.2 %copy-start = (f32[512,256]{1,0:T(8,128)S(1)}, f32[512,256]{1,0:T(8,128)}, u32[]{:S(2)}) copy-start(f32[512,256]{1,0:T(8,128)} %get-tuple-element.21) | copy-start | bytes 1572868
  85.1 9.0 %copy-start.2 = (f32[128,256]{1,0:T(8,128)S(1)}, f32[128,256]{1,0:T(8,128)}, u32[]{:S(2)}) copy-start(f32[128,256]{1,0:T(8,128)} %get-tuple-element.22) | copy-start | bytes 393220
  85.1 9.7 %copy-start.1 = (f32[128,256]{1,0:T(8,128)S(1)}, f32[128,256]{1,0:T(8,128)}, u32[]{:S(2)}) copy-start(f32[128,256]{1,0:T(8,128)} %get-tuple-element.23) | copy-start | bytes 393220

commit v2 on v1

v2 whole, which is shorter than its diff:
```python
import jax
import jax.numpy as jnp
from jax import lax
from jax.experimental import pallas as pl
from jax.experimental.pallas import tpu as pltpu
from jax.sharding import PartitionSpec as P

MESH = pl.DeviceIdType.MESH
HD = 128
SCALE = HD ** -0.5
ROWS = 256
F32 = jnp.float32
BF16 = jnp.bfloat16


def nn(a, b):
    return jnp.dot(a, b, preferred_element_type=F32)


def nt(a, b):
    return lax.dot_general(a, b, (((1,), (1,)), ((), ())), preferred_element_type=F32)


def kernel(
    tok_h, wq_h, ctx_h, wk_h, wv_h, sq_h, sk_h, sv_h, gs_h, gc_h,
    o_self, o_dsq, o_dsk, o_dsv, o_cross, o_gwq, o_gwk, o_gwv,
    tok, wq, wkv, wkvt, own, gc, ctx, kvt, wst, dpst, mst, dkvt,
    cm, cl, cacc, sst, sm, sl, sacc, blk, stat, tb, dqt, wown, wmine, wpeer, wz,
    lsem, ssem, ctx_sem, sib_sem, blk_sem, stat_sem, tok_sem, tokg_sem, tsib_sem, dq_sem, wp_sem,
    wz_sem,
):
    e = lax.axis_index("enc")
    d = lax.axis_index("dec")
    y, low = e // 4, e % 4
    core = e % 2
    yup = lax.rem(y + 1, 4) * 4 + low
    ydn = lax.rem(y + 3, 4) * 4 + low
    yfar = lax.rem(y + 2, 4) * 4 + low
    sib = e + 1 - 2 * core
    xflip = e + 2 - 4 * ((e // 2) % 2)
    xh = d // 4

    def peer(m):
        out = d
        for bit in (1, 2, 4):
            if m & bit:
                out = out + bit - 2 * bit * ((d // bit) % 2)
        return out

    dev = {
        "yup": (yup, d), "ydn": (ydn, d), "yfar": (yfar, d), "sib": (sib, d),
        "xi": (xflip, d), "xo": (xflip, peer(4)),
    }
    partner = [(e, peer(m)) for m in range(8)]

    barrier = pltpu.get_barrier_semaphore()
    greet = list(dev.values()) + partner[1:]
    for target in greet:
        pl.semaphore_signal(barrier, inc=1, device_id=target, device_id_type=MESH)

    loads = []

    def load(src, dst):
        copy = pltpu.make_async_copy(src, dst, lsem.at[len(loads)])
        copy.start()
        loads.append(copy)
        return copy

    l_own = [load(r, own.at[i]) for i, r in enumerate((sk_h, sv_h, sq_h, gs_h))]
    l_ctx = load(ctx_h, ctx.at[0, 0])
    l_wk = load(wk_h, wkv.at[:, pl.ds(0, ROWS)])
    l_wv = load(wv_h, wkv.at[:, pl.ds(ROWS, ROWS)])
    l_gc = load(gc_h, gc)
    l_tok = load(tok_h, tok)
    l_wq = load(wq_h, wq)

    sends = []

    def send(src, dst, rsem, target):
        copy = pltpu.make_async_remote_copy(
            src_ref=src, dst_ref=dst, send_sem=ssem.at[len(sends)], recv_sem=rsem,
            device_id=target, device_id_type=MESH,
        )
        copy.start()
        sends.append(copy)

    def arrived(dst, rsem):
        pltpu.make_async_remote_copy(
            src_ref=dst, dst_ref=dst, send_sem=ssem.at[0], recv_sem=rsem,
            device_id=dev["sib"], device_id_type=MESH,
        ).wait_recv()

    quarter = ROWS // 4

    def part(k, i, side=0):
        return ctx.at[k, side, pl.ds(i * quarter, quarter), :]

    def pass_on(src, k, i, target):
        send(src, part(k, i), ctx_sem.at[k, i], target)

    def got(k, i):
        arrived(part(k, i), ctx_sem.at[k, i])

    def share(k, i):
        send(part(k, i), part(k, i, 1), sib_sem.at[k, i], dev["sib"])

    def shared(k):
        for i in range(4):
            arrived(part(k, i, 1), sib_sem.at[k, i])

    for c in l_own:
        c.wait()
    l_ctx.wait()
    pl.semaphore_wait(barrier, len(greet))

    def own_block(m):
        bit = (d // (1 if m == 1 else 2 if m < 4 else 4)) % 2
        return own.at[pl.ds(2 * bit, 2)]

    def blk_out(m, slot, src):
        send(src, blk.at[slot], blk_sem.at[slot], partner[m])

    blk_out(4, 4, own_block(4))
    for i in (0, 1):
        pass_on(part(0, i), 6, i, dev["yup"])
        pass_on(part(0, 2 + i), 2, 2 + i, dev["ydn"])
        pass_on(part(0, i), 1, i, dev["xi"])
        pass_on(part(0, 2 + i), 1, 2 + i, dev["xo"])
    for i in range(4):
        share(0, i)
    for i in (0, 1):
        pass_on(part(0, 2 + i), 6, 2 + i, dev["yup"])
        pass_on(part(0, i), 2, i, dev["ydn"])
    blk_out(1, 1, own_block(1))
    blk_out(3, 3, own_block(3))
    blk_out(2, 2, own_block(2))

    l_wk.wait()
    l_wv.wait()
    wkvt[...] = wkv[...].T
    l_tok.wait()
    l_wq.wait()
    cq = nn(tok[...], wq[...]).astype(BF16)
    cqt = cq.T
    l_gc.wait()
    gcv = gc[...]
    gct = gcv.T

    def hs(h):
        return slice(h * HD, (h + 1) * HD)

    def cross_forward(k, first):
        x = ctx[k].reshape(2 * ROWS, ctx.shape[3])
        kv = nt(wkvt[...], x).astype(BF16)
        cols = slice(k * 2 * ROWS, (k + 1) * 2 * ROWS)
        kvt[:, cols] = kv
        for h in range(2):
            s = nn(cq[:, hs(h)], kv[hs(h)]) * SCALE
            top = jnp.max(s, axis=1, keepdims=True)
            if not first:
                old = cm[h]
                top = jnp.maximum(old, top)
            w = jnp.exp(s - top)
            wst[h, :, cols] = w
            dpst[h, :, cols] = nn(gcv[:, hs(h)], kv[hs(2 + h)])
            add_l = jnp.sum(w, axis=1, keepdims=True)
            add_o = nt(w.astype(BF16), kv[hs(2 + h)])
            if not first:
                fix = jnp.exp(old - top)
                add_l = add_l + cl[h] * fix
                add_o = add_o + cacc[h] * fix
            cm[h] = top
            cl[h] = add_l
            cacc[h] = add_o
            mst[k, h] = top

    row = lax.broadcasted_iota(jnp.int32, (ROWS, ROWS), 0)
    col = lax.broadcasted_iota(jnp.int32, (ROWS, ROWS), 1)

    def xor_slot(p):
        out = 0
        for bit in (1, 2, 4):
            out = out + bit * (((d // bit) + (p // bit)) % 2)
        return out

    def halves(f, x):
        return f(x[:, :HD], x[:, HD:])

    def self_scores(p, carry):
        slot = xor_slot(p)
        for h in range(2):
            s = nt(own[2, :, hs(h)], blk[slot, 0, :, hs(h)]) * SCALE
            sst[slot, h] = s
            sm[h] = jnp.maximum(sm[h], halves(jnp.maximum, s))
        return carry

    shared(0)
    cross_forward(0, True)
    for i in (0, 1):
        got(6, i)
        pass_on(part(6, i), 4, i, dev["yup"])
        pass_on(part(6, i), 7, i, dev["xi"])
        share(6, i)
        got(2, 2 + i)
        pass_on(part(2, 2 + i), 4, 2 + i, dev["ydn"])
        pass_on(part(2, 2 + i), 3, 2 + i, dev["xo"])
        share(2, 2 + i)
    for i in range(4):
        got(1, i)
        share(1, i)
    for h in range(2):
        s = jnp.where(row >= col, nt(own[2, :, hs(h)], own[0, :, hs(h)]) * SCALE, -1e30)
        sst[0, h] = s
        sm[h] = halves(jnp.maximum, s)
    arrived(blk.at[4], blk_sem.at[4])
    for m in (1, 3, 2):
        blk_out(m, 4 + m, blk.at[4])
    shared(1)
    cross_forward(1, False)
    for i in (0, 1):
        got(6, 2 + i)
        pass_on(part(6, 2 + i), 7, 2 + i, dev["xo"])
        share(6, 2 + i)
        got(2, i)
        pass_on(part(2, i), 3, i, dev["xi"])
        share(2, i)
    lane = (y * 2 + core) * 32
    trows = pl.ds(pl.multiple_of(lane, 32), 32)

    def tcols(p):
        return pl.ds(pl.multiple_of(p * 512, 512), 512)

    for m in range(1, 8):
        send(tok.at[trows, tcols(partner[m][1])], tb.at[m, trows], tok_sem.at[m], partner[m])
    l_tb = load(tok.at[:, tcols(d)], tb.at[0])
    shared(6)
    cross_forward(6, False)
    for i in (0, 1):
        got(7, i)
        pass_on(part(7, i), 5, i, dev["yup"])
        share(7, i)
        got(3, 2 + i)
        pass_on(part(3, 2 + i), 5, 2 + i, dev["ydn"])
        share(3, 2 + i)
    shared(2)
    cross_forward(2, False)
    for m in (1, 2, 3):
        arrived(blk.at[m], blk_sem.at[m])
    lax.fori_loop(4 * xh, d, self_scores, 0)
    for i in range(4):
        got(4, i)
        share(4, i)
    shared(4)
    cross_forward(4, False)
    for i in (0, 1):
        got(7, 2 + i)
        share(7, 2 + i)
        got(3, i)
        share(3, i)
    shared(7)
    cross_forward(7, False)
    shared(3)
    cross_forward(3, False)
    for m in range(1, 8):
        arrived(tb.at[m, trows], tok_sem.at[m])
    l_tb.wait()

    def trange(ee):
        return pl.ds(pl.multiple_of((ee // 4 * 2 + ee % 2) * 32, 32), 32)

    moved = tb.at[pl.ds(1, 7), trows]
    for i, name in enumerate(("yup", "ydn", "yfar", "sib")):
        send(moved, moved, tokg_sem.at[i], dev[name])
    for i in range(4):
        got(5, i)
        share(5, i)
    for m in (5, 6, 7):
        arrived(blk.at[m], blk_sem.at[m])
    lax.fori_loop(0, 4 * xh, self_scores, 0)
    tops = [jnp.max(sm[h], axis=1, keepdims=True) for h in range(2)]
    for h in range(2):
        w = jnp.exp(sst[0, h] - tops[h])
        sl[h] = halves(jnp.add, w)
        sacc[h] = nn(w.astype(BF16), own[1, :, hs(h)])
        sm[h] = jnp.broadcast_to(tops[h], (ROWS, HD))

    def self_weights(p, carry):
        slot = xor_slot(p)
        for h in range(2):
            w = jnp.exp(sst[slot, h] - sm[h, :, 0:1])
            sl[h] += halves(jnp.add, w)
            sacc[h] += nn(w.astype(BF16), blk[slot, 1, :, hs(h)])
        return carry

    lax.fori_loop(0, d, self_weights, 0)
    for h in range(2):
        norm = jnp.sum(sl[h], axis=1, keepdims=True)
        out = (sacc[h] / norm).astype(BF16)
        o_self[:, hs(h)] = out
        g = own[3, :, hs(h)]
        lse = tops[h] + jnp.log(norm)
        delta = jnp.sum(g.astype(F32) * out.astype(F32), axis=1, keepdims=True)
        sm[h] = jnp.broadcast_to(lse, (ROWS, HD))
        sl[h] = jnp.broadcast_to(delta, (ROWS, HD))
        stat[0, 2 * h:2 * h + 1, :] = sm[h].T[0:1]
        stat[0, 2 * h + 1:2 * h + 2, :] = sl[h].T[0:1]
    for m in range(1, 8):
        send(stat.at[0], stat.at[m], stat_sem.at[m], partner[m])
    shared(5)
    cross_forward(5, False)

    def weight_part(h, group):
        cols = pl.ds(pl.multiple_of(group * 512, 512), 512)
        return nn(dkvt[h], ctx.reshape(16 * ROWS, ctx.shape[3])[:, cols])

    def dq_slot(m, h):
        return dqt.at[m, pl.ds(h * HD, HD), :]

    for h in range(2):
        norm = cl[h]
        out = (cacc[h] / norm).astype(BF16)
        o_cross[:, hs(h)] = out
        g = gcv[:, hs(h)]
        lse = cm[h] + jnp.log(norm)
        delta = jnp.sum(g.astype(F32) * out.astype(F32), axis=1, keepdims=True)
        qt = cqt[hs(h)]
        gt = gct[hs(h)]
        dq = None
        for k in range(8):
            cols = slice(k * 2 * ROWS, (k + 1) * 2 * ROWS)
            p = wst[h, :, cols] * jnp.exp(mst[k, h] - lse)
            ds = (p * (dpst[h, :, cols] - delta) * SCALE).astype(BF16)
            add = nt(ds, kvt[hs(h), cols])
            dq = add if dq is None else dq + add
            dkvt[h, 0:HD, cols] = nn(qt, ds).astype(BF16)
            dkvt[h, HD:, cols] = nn(gt, p.astype(BF16)).astype(BF16)
        dqt[0, hs(h), :] = dq.astype(BF16).T
        for m in (4, 1, 3, 2):
            send(dq_slot(0, h), dq_slot(m, h), dq_sem.at[m, h], partner[m])
        piece = weight_part(h, 1 - xh).astype(BF16)
        for z in range(4):
            wmine[h, z] = piece[:, z * HD:(z + 1) * HD]
        send(wmine.at[h], wpeer.at[h], wp_sem.at[h], partner[4])

    def forward_dq(h):
        arrived(dq_slot(4, h), dq_sem.at[4, h])
        for m in (1, 3, 2):
            send(dq_slot(4, h), dq_slot(4 + m, h), dq_sem.at[4 + m, h], partner[m])

    forward_dq(0)
    for h in range(2):
        piece = weight_part(h, xh)
        for z in range(4):
            wown[h, z] = piece[:, z * HD:(z + 1) * HD]
    for i, ee in enumerate((ydn, yup, yfar, sib)):
        arrived(tb.at[pl.ds(1, 7), trange(ee)], tokg_sem.at[i])
    for i, ee in enumerate((ydn, yup, yfar)):
        spot = tb.at[pl.ds(1, 7), trange(ee)]
        send(spot, spot, tsib_sem.at[i], dev["sib"])
    forward_dq(1)

    def sum_and_pass(h):
        arrived(wpeer.at[h], wp_sem.at[h])
        wown[h] = wown[h] + wpeer[h].astype(F32)
        wpeer[h] = wown[h].astype(BF16)
        for m in (1, 3, 2):
            send(
                wpeer.at[h, partner[m][1] - 4 * xh], wz.at[m, h], wz_sem.at[m, h], partner[m]
            )

    sum_and_pass(0)

    def query_grad(h, s, v, k):
        p = jnp.exp(s - sm[h, :, 0:1])
        dp = nt(own[3, :, hs(h)], v)
        return nn((p * (dp - sl[h, :, 0:1]) * SCALE).astype(BF16), k)

    for h in range(2):
        o_dsq[:, hs(h)] = query_grad(h, sst[0, h], own[1, :, hs(h)], own[0, :, hs(h)])

    def self_query(p, carry):
        slot = xor_slot(p)
        for h in range(2):
            o_dsq[:, hs(h)] += query_grad(
                h, sst[slot, h], blk[slot, 1, :, hs(h)], blk[slot, 0, :, hs(h)]
            )
        return carry

    lax.fori_loop(0, d, self_query, 0)

    def key_grad(h, st, q, g, lse, delta):
        p = jnp.exp(st - lse)
        dp = nt(own[1, :, hs(h)], g)
        ds = (p * (dp - delta) * SCALE).astype(BF16)
        return nn(ds, q), nn(p.astype(BF16), g)

    for h in range(2):
        q, g = own[2, :, hs(h)], own[3, :, hs(h)]
        st = jnp.where(col >= row, nt(own[0, :, hs(h)], q) * SCALE, -1e30)
        dk, dv = key_grad(h, st, q, g, stat[0, 2 * h:2 * h + 1], stat[0, 2 * h + 1:2 * h + 2])
        o_dsk[:, hs(h)] = dk
        o_dsv[:, hs(h)] = dv
    for m in range(1, 8):
        arrived(stat.at[m], stat_sem.at[m])

    def self_key(p, carry):
        slot = xor_slot(p)
        for h in range(2):
            q, g = blk[slot, 0, :, hs(h)], blk[slot, 1, :, hs(h)]
            st = nt(own[0, :, hs(h)], q) * SCALE
            dk, dv = key_grad(
                h, st, q, g, stat[slot, 2 * h:2 * h + 1], stat[slot, 2 * h + 1:2 * h + 2]
            )
            o_dsk[:, hs(h)] += dk
            o_dsv[:, hs(h)] += dv
        return carry

    lax.fori_loop(d + 1, 8, self_key, 0)
    sum_and_pass(1)

    for i, ee in enumerate((ydn, yup, yfar)):
        ss = ee + 1 - 2 * core
        arrived(tb.at[pl.ds(1, 7), trange(ss)], tsib_sem.at[i])
    for m in (1, 2, 3, 5, 6, 7):
        for h in range(2):
            arrived(dq_slot(m, h), dq_sem.at[m, h])
    gw = None
    for m in range(8):
        add = nn(dqt[m], tb[m])
        gw = add if gw is None else gw + add
    o_gwq[...] = gw.T
    for m in (1, 2, 3):
        for h in range(2):
            arrived(wz.at[m, h], wz_sem.at[m, h])
    mine = d - 4 * xh
    for h in range(2):
        total = wown[h, mine]
        for m in (1, 2, 3):
            total = total + wz[m, h].astype(F32)
        o_gwk[:, hs(h)] = total[0:HD].T
        o_gwv[:, hs(h)] = total[HD:].T

    for copy in sends:
        copy.wait_send()


def hand_over(*refs):
    sources, targets, held, sem = refs[:8], refs[8:16], refs[16:24], refs[24]
    loads = [
        pltpu.make_async_copy(a, b, sem.at[0, i]) for i, (a, b) in enumerate(zip(sources, held))
    ]
    stores = [
        pltpu.make_async_copy(a, b, sem.at[1, i]) for i, (a, b) in enumerate(zip(held, targets))
    ]
    for copy in loads:
        copy.start()
    for copy, store in zip(loads, stores):
        copy.wait()
        store.start()
    for store in stores:
        store.wait()


def body(*args):
    vm, any_ = pl.BlockSpec(memory_space=pltpu.VMEM), pl.BlockSpec(memory_space=pl.ANY)
    shape = jax.ShapeDtypeStruct
    block = (ROWS, ROWS)
    dma = pltpu.SemaphoreType.DMA
    shapes = (
        shape(block, BF16), shape(block, F32), shape(block, F32), shape(block, F32),
        shape(block, BF16), shape((512, ROWS), F32), shape((128, ROWS), F32),
        shape((128, ROWS), F32),
    )
    results = pl.pallas_call(
        kernel,
        out_shape=shapes,
        in_specs=[any_] * 10,
        out_specs=[vm] * 8,
        scratch_shapes=[
            pltpu.VMEM((256, 4096), BF16),
            pltpu.VMEM((4096, 256), BF16),
            pltpu.VMEM((1024, 512), BF16),
            pltpu.VMEM((512, 1024), BF16),
            pltpu.VMEM((4, 256, 256), BF16),
            pltpu.VMEM((256, 256), BF16),
            pltpu.VMEM((8, 2, 256, 1024), BF16),
            pltpu.VMEM((512, 4096), BF16),
            pltpu.VMEM((2, 256, 4096), F32),
            pltpu.VMEM((2, 256, 4096), F32),
            pltpu.VMEM((8, 2, 256, 1), F32),
            pltpu.VMEM((2, 256, 4096), BF16),
            pltpu.VMEM((2, 256, 1), F32),
            pltpu.VMEM((2, 256, 1), F32),
            pltpu.VMEM((2, 256, 128), F32),
            pltpu.VMEM((8, 2, 256, 256), F32),
            pltpu.VMEM((2, 256, 128), F32),
            pltpu.VMEM((2, 256, 128), F32),
            pltpu.VMEM((2, 256, 128), F32),
            pltpu.VMEM((8, 2, 256, 256), BF16),
            pltpu.VMEM((8, 8, 256), F32),
            pltpu.VMEM((8, 256, 512), BF16),
            pltpu.VMEM((8, 256, 256), BF16),
            pltpu.VMEM((2, 4, 256, 128), F32),
            pltpu.VMEM((2, 4, 256, 128), BF16),
            pltpu.VMEM((2, 4, 256, 128), BF16),
            pltpu.VMEM((4, 2, 256, 128), BF16),
            dma((16,)), dma((128,)), dma((8, 4)), dma((8, 4)), dma((8,)), dma((8,)), dma((8,)),
            dma((4,)), dma((3,)), dma((8, 2)), dma((2,)), dma((4, 2)),
        ],
        compiler_params=pltpu.CompilerParams(
            collective_id=0, has_side_effects=True, vmem_limit_bytes=62 << 20
        ),
        name="layer",
    )(*args)
    return tuple(pl.pallas_call(
        hand_over,
        out_shape=shapes,
        in_specs=[any_] * 8,
        out_specs=[any_] * 8,
        scratch_shapes=[pltpu.VMEM(x.shape, x.dtype) for x in shapes] + [dma((2, 8))],
        name="hand_over",
    )(*results))


def solution(mesh):
    placed = (
        P("dec", None), P(None, "enc"), P("enc", None), P(None, "enc"), P(None, "enc"),
    ) + (P("dec", "enc"),) * 5
    return jax.shard_map(
        body, mesh=mesh, in_specs=placed, out_specs=(P("dec", "enc"),) * 8, check_vma=False
    )
```

time: 95.7 us -> 73.1 us (0.76)
  the two profiles are of different devices: /device:TPU:25 before, /device:TPU:0 now
where the time goes in v2:
time: 73.1 us; the launch traced here: 73 us
  Pallas kernels  72.2 us (99%)
  between operations  0.81 us (1%)
    pallas_call x1, Pallas kernels, body(): pl.pallas_call(kernel, out_shape=shapes, in_specs=[any_] * 10, out_specs=...  69.8 us
    pallas_call x1, Pallas kernels, body(): pl.pallas_call(hand_over, out_shape=shapes, in_specs=[any_] * 8, out_spec...  2.41 us

profile of v2, /device:TPU:0, one launch (start us, length us, event | category | flops | bytes accessed | tf_op | source)
XLA Modules:
  0.0 73.0 jit_solution(3438283379692935113)
XLA Ops:
  0.6 69.8 %layer.1 = (bf16[256,256]{1,0:T(8,128)(2,1)}, f32[256,256]{1,0:T(8,128)}, f32[256,256]{1,0:T(8,128)}, f32[256,256]{1,0:T(8,128)}, bf16[256,256]{1,0:T(8,128)(2,1...) custom-call(bf16[256,4096]{1,0:T(8,128)(2,1)} %tok_h.1, bf16[4096,256]{1,0:T(8,128)(2,1)} %wq_h.1, ...), custom_call_target="tpu_custom_call" | custom-call | tf_op jit(solution)/shard_map/layer/pallas_call | solution.py:474
  70.4 2.4 %hand_over.1 = (bf16[256,256]{1,0:T(8,128)(2,1)}, f32[256,256]{1,0:T(8,128)}, f32[256,256]{1,0:T(8,128)}, f32[256,256]{1,0:T(8,128)}, bf16[256,256]{1,0:T(8,128)...) custom-call(bf16[256,256]{1,0:T(8,128)(2,1)} %get-tuple-element.16.refs_0_, ...), custom_call_target="tpu_custom_call" | custom-call | tf_op jit(solution)/shard_map/hand_over/pallas_call | solution.py:515

commit v3 on v2

--- a/solution.py
+++ b/solution.py
@@ -25,7 +25,7 @@
     tok_h, wq_h, ctx_h, wk_h, wv_h, sq_h, sk_h, sv_h, gs_h, gc_h,
     o_self, o_dsq, o_dsk, o_dsv, o_cross, o_gwq, o_gwk, o_gwv,
     tok, wq, wkv, wkvt, own, gc, ctx, kvt, wst, dpst, mst, dkvt,
-    cm, cl, cacc, sst, sm, sl, sacc, blk, stat, tb, dqt, wown, wmine, wpeer, wz,
+    prob, dscore, cm, cl, cacc, st_top, sst, sm, sl, sacc, blk, stat, tb, dqt, wown, wmine, wpeer, wz,
     lsem, ssem, ctx_sem, sib_sem, blk_sem, stat_sem, tok_sem, tokg_sem, tsib_sem, dq_sem, wp_sem,
     wz_sem,
 ):
@@ -67,7 +67,7 @@
         return copy
 
     l_own = [load(r, own.at[i]) for i, r in enumerate((sk_h, sv_h, sq_h, gs_h))]
-    l_ctx = load(ctx_h, ctx.at[0, 0])
+    l_ctx = [load(ctx_h.at[pl.ds(a * 128, 128)], ctx.at[0, a, 0]) for a in range(2)]
     l_wk = load(wk_h, wkv.at[:, pl.ds(0, ROWS)])
     l_wv = load(wv_h, wkv.at[:, pl.ds(ROWS, ROWS)])
     l_gc = load(gc_h, gc)
@@ -93,7 +93,7 @@
     quarter = ROWS // 4
 
     def part(k, i, side=0):
-        return ctx.at[k, side, pl.ds(i * quarter, quarter), :]
+        return ctx.at[k, i // 2, side, pl.ds(i % 2 * quarter, quarter), :]
 
     def pass_on(src, k, i, target):
         send(src, part(k, i), ctx_sem.at[k, i], target)
@@ -110,7 +110,8 @@
 
     for c in l_own:
         c.wait()
-    l_ctx.wait()
+    for c in l_ctx:
+        c.wait()
     pl.semaphore_wait(barrier, len(greet))
 
     def own_block(m):
@@ -122,18 +123,17 @@
 
     blk_out(4, 4, own_block(4))
     for i in (0, 1):
+        pass_on(part(0, i), 1, i, dev["xi"])
+        pass_on(part(0, 2 + i), 1, 2 + i, dev["xo"])
         pass_on(part(0, i), 6, i, dev["yup"])
         pass_on(part(0, 2 + i), 2, 2 + i, dev["ydn"])
-        pass_on(part(0, i), 1, i, dev["xi"])
-        pass_on(part(0, 2 + i), 1, 2 + i, dev["xo"])
     for i in range(4):
         share(0, i)
     for i in (0, 1):
         pass_on(part(0, 2 + i), 6, 2 + i, dev["yup"])
         pass_on(part(0, i), 2, i, dev["ydn"])
-    blk_out(1, 1, own_block(1))
-    blk_out(3, 3, own_block(3))
-    blk_out(2, 2, own_block(2))
+    for m in (1, 3, 2):
+        blk_out(m, m, own_block(m))
 
     l_wk.wait()
     l_wv.wait()
@@ -149,30 +149,51 @@
     def hs(h):
         return slice(h * HD, (h + 1) * HD)
 
-    def cross_forward(k, first):
-        x = ctx[k].reshape(2 * ROWS, ctx.shape[3])
-        kv = nt(wkvt[...], x).astype(BF16)
-        cols = slice(k * 2 * ROWS, (k + 1) * 2 * ROWS)
-        kvt[:, cols] = kv
-        for h in range(2):
-            s = nn(cq[:, hs(h)], kv[hs(h)]) * SCALE
-            top = jnp.max(s, axis=1, keepdims=True)
-            if not first:
-                old = cm[h]
-                top = jnp.maximum(old, top)
-            w = jnp.exp(s - top)
-            wst[h, :, cols] = w
-            dpst[h, :, cols] = nn(gcv[:, hs(h)], kv[hs(2 + h)])
-            add_l = jnp.sum(w, axis=1, keepdims=True)
-            add_o = nt(w.astype(BF16), kv[hs(2 + h)])
-            if not first:
-                fix = jnp.exp(old - top)
+    ctx2 = ctx.reshape(16 * ROWS, ctx.shape[4])
+
+    def span(k):
+        return slice(k * 2 * ROWS, (k + 1) * 2 * ROWS)
+
+    def lanes(f, x):
+        out = x[:, :HD]
+        for i in range(1, x.shape[1] // HD):
+            out = f(out, x[:, i * HD:(i + 1) * HD])
+        return out
+
+    def cross_scores(k, first=False):
+        cols = span(k)
+        x = ctx2[cols]
+        kv = [nt(wkvt[i * ROWS:(i + 1) * ROWS], x).astype(BF16) for i in range(2)]
+        for i in range(2):
+            kvt[i * ROWS:(i + 1) * ROWS, cols] = kv[i]
+        for h in range(2):
+            s = nn(cq[:, hs(h)], kv[0][hs(h)]) * SCALE
+            wst[h, :, cols] = s
+            top = lanes(jnp.maximum, s)
+            cm[h] = top if first else jnp.maximum(cm[h], top)
+            dpst[h, :, cols] = nn(gcv[:, hs(h)], kv[1][hs(h)])
+
+    def cross_weights(g, chunks):
+        for h in range(2):
+            top = jnp.max(cm[h], axis=1, keepdims=True)
+            mst[g, h] = top
+            add_l, add_o = None, None
+            for k in chunks:
+                cols = span(k)
+                w = jnp.exp(wst[h, :, cols] - top)
+                wst[h, :, cols] = w
+                one_l = lanes(jnp.add, w)
+                one_o = nt(w.astype(BF16), kvt[ROWS + h * HD:ROWS + (h + 1) * HD, cols])
+                add_l = one_l if add_l is None else add_l + one_l
+                add_o = one_o if add_o is None else add_o + one_o
+            if g:
+                fix = jnp.exp(mst[g - 1, h] - top)
                 add_l = add_l + cl[h] * fix
                 add_o = add_o + cacc[h] * fix
-            cm[h] = top
             cl[h] = add_l
             cacc[h] = add_o
-            mst[k, h] = top
+
+    groups = ((0, 1), (6, 2), (4, 7, 3), (5,))
 
     row = lax.broadcasted_iota(jnp.int32, (ROWS, ROWS), 0)
     col = lax.broadcasted_iota(jnp.int32, (ROWS, ROWS), 1)
@@ -194,47 +215,55 @@
             sm[h] = jnp.maximum(sm[h], halves(jnp.maximum, s))
         return carry
 
+    def self_weights(p, carry):
+        slot = xor_slot(p)
+        for h in range(2):
+            w = jnp.exp(sst[slot, h] - st_top[h])
+            sl[h] += halves(jnp.add, w)
+            sacc[h] += nn(w.astype(BF16), blk[slot, 1, :, hs(h)])
+        return carry
+
     shared(0)
-    cross_forward(0, True)
-    for i in (0, 1):
-        got(6, i)
-        pass_on(part(6, i), 4, i, dev["yup"])
-        pass_on(part(6, i), 7, i, dev["xi"])
-        share(6, i)
-        got(2, 2 + i)
-        pass_on(part(2, 2 + i), 4, 2 + i, dev["ydn"])
-        pass_on(part(2, 2 + i), 3, 2 + i, dev["xo"])
-        share(2, 2 + i)
+    cross_scores(0, True)
+    got_up = lambda i: (
+        got(6, i),
+        pass_on(part(6, i), 4, i, dev["yup"]) if i < 2 else None,
+        pass_on(part(6, i), 7, i, dev["xi"] if i < 2 else dev["xo"]),
+        share(6, i),
+    )
+    got_down = lambda i: (
+        got(2, i),
+        pass_on(part(2, i), 4, i, dev["ydn"]) if i > 1 else None,
+        pass_on(part(2, i), 3, i, dev["xi"] if i < 2 else dev["xo"]),
+        share(2, i),
+    )
+    got_up(0)
+    got_down(2)
+    for h in range(2):
+        s = jnp.where(row >= col, nt(own[2, :, hs(h)], own[0, :, hs(h)]) * SCALE, -1e30)
+        sst[0, h] = s
+        sm[h] = halves(jnp.maximum, s)
+    got_up(1)
+    got_down(3)
+    arrived(blk.at[4], blk_sem.at[4])
+    for m in (1, 3, 2):
+        blk_out(m, 4 + m, blk.at[4])
+    got_up(2)
+    got_down(0)
+    got_up(3)
+    got_down(1)
+    shared(6)
+    cross_scores(6)
     for i in range(4):
         got(1, i)
         share(1, i)
-    for h in range(2):
-        s = jnp.where(row >= col, nt(own[2, :, hs(h)], own[0, :, hs(h)]) * SCALE, -1e30)
-        sst[0, h] = s
-        sm[h] = halves(jnp.maximum, s)
-    arrived(blk.at[4], blk_sem.at[4])
-    for m in (1, 3, 2):
-        blk_out(m, 4 + m, blk.at[4])
+    shared(2)
+    cross_scores(2)
     shared(1)
-    cross_forward(1, False)
-    for i in (0, 1):
-        got(6, 2 + i)
-        pass_on(part(6, 2 + i), 7, 2 + i, dev["xo"])
-        share(6, 2 + i)
-        got(2, i)
-        pass_on(part(2, i), 3, i, dev["xi"])
-        share(2, i)
-    lane = (y * 2 + core) * 32
-    trows = pl.ds(pl.multiple_of(lane, 32), 32)
-
-    def tcols(p):
-        return pl.ds(pl.multiple_of(p * 512, 512), 512)
-
-    for m in range(1, 8):
-        send(tok.at[trows, tcols(partner[m][1])], tb.at[m, trows], tok_sem.at[m], partner[m])
-    l_tb = load(tok.at[:, tcols(d)], tb.at[0])
-    shared(6)
-    cross_forward(6, False)
+    cross_scores(1)
+    for m in (1, 2, 3):
+        arrived(blk.at[m], blk_sem.at[m])
+    lax.fori_loop(4 * xh, d, self_scores, 0)
     for i in (0, 1):
         got(7, i)
         pass_on(part(7, i), 5, i, dev["yup"])
@@ -242,101 +271,72 @@
         got(3, 2 + i)
         pass_on(part(3, 2 + i), 5, 2 + i, dev["ydn"])
         share(3, 2 + i)
-    shared(2)
-    cross_forward(2, False)
-    for m in (1, 2, 3):
-        arrived(blk.at[m], blk_sem.at[m])
-    lax.fori_loop(4 * xh, d, self_scores, 0)
     for i in range(4):
         got(4, i)
         share(4, i)
+    cross_weights(0, groups[0])
+    cross_weights(1, groups[1])
+    for h in range(2):
+        top = jnp.max(sm[h], axis=1, keepdims=True)
+        st_top[h] = top
+        w = jnp.exp(sst[0, h] - top)
+        sl[h] = halves(jnp.add, w)
+        sacc[h] = nn(w.astype(BF16), own[1, :, hs(h)])
+    lax.fori_loop(4 * xh, d, self_weights, 0)
     shared(4)
-    cross_forward(4, False)
+    cross_scores(4)
     for i in (0, 1):
         got(7, 2 + i)
         share(7, 2 + i)
         got(3, i)
         share(3, i)
     shared(7)
-    cross_forward(7, False)
-    shared(3)
-    cross_forward(3, False)
-    for m in range(1, 8):
-        arrived(tb.at[m, trows], tok_sem.at[m])
-    l_tb.wait()
-
-    def trange(ee):
-        return pl.ds(pl.multiple_of((ee // 4 * 2 + ee % 2) * 32, 32), 32)
-
-    moved = tb.at[pl.ds(1, 7), trows]
-    for i, name in enumerate(("yup", "ydn", "yfar", "sib")):
-        send(moved, moved, tokg_sem.at[i], dev[name])
+    cross_scores(7)
     for i in range(4):
         got(5, i)
         share(5, i)
-    for m in (5, 6, 7):
-        arrived(blk.at[m], blk_sem.at[m])
-    lax.fori_loop(0, 4 * xh, self_scores, 0)
-    tops = [jnp.max(sm[h], axis=1, keepdims=True) for h in range(2)]
-    for h in range(2):
-        w = jnp.exp(sst[0, h] - tops[h])
-        sl[h] = halves(jnp.add, w)
-        sacc[h] = nn(w.astype(BF16), own[1, :, hs(h)])
-        sm[h] = jnp.broadcast_to(tops[h], (ROWS, HD))
-
-    def self_weights(p, carry):
-        slot = xor_slot(p)
-        for h in range(2):
-            w = jnp.exp(sst[slot, h] - sm[h, :, 0:1])
-            sl[h] += halves(jnp.add, w)
-            sacc[h] += nn(w.astype(BF16), blk[slot, 1, :, hs(h)])
-        return carry
-
-    lax.fori_loop(0, d, self_weights, 0)
-    for h in range(2):
-        norm = jnp.sum(sl[h], axis=1, keepdims=True)
-        out = (sacc[h] / norm).astype(BF16)
-        o_self[:, hs(h)] = out
-        g = own[3, :, hs(h)]
-        lse = tops[h] + jnp.log(norm)
-        delta = jnp.sum(g.astype(F32) * out.astype(F32), axis=1, keepdims=True)
-        sm[h] = jnp.broadcast_to(lse, (ROWS, HD))
-        sl[h] = jnp.broadcast_to(delta, (ROWS, HD))
-        stat[0, 2 * h:2 * h + 1, :] = sm[h].T[0:1]
-        stat[0, 2 * h + 1:2 * h + 2, :] = sl[h].T[0:1]
+    shared(3)
+    cross_scores(3)
+    lane = (y * 2 + core) * 32
+    trows = pl.ds(pl.multiple_of(lane, 32), 32)
+
+    def tcols(p):
+        return pl.ds(pl.multiple_of(p * 512, 512), 512)
+
     for m in range(1, 8):
-        send(stat.at[0], stat.at[m], stat_sem.at[m], partner[m])
+        send(tok.at[trows, tcols(partner[m][1])], tb.at[m, trows], tok_sem.at[m], partner[m])
+    l_tb = load(tok.at[:, tcols(d)], tb.at[0])
+    cross_weights(2, groups[2])
     shared(5)
-    cross_forward(5, False)
+    cross_scores(5)
+    cross_weights(3, groups[3])
 
     def weight_part(h, group):
-        cols = pl.ds(pl.multiple_of(group * 512, 512), 512)
-        return nn(dkvt[h], ctx.reshape(16 * ROWS, ctx.shape[3])[:, cols])
+        return nn(dkvt[h], ctx2[:, pl.ds(pl.multiple_of(group * 512, 512), 512)])
 
     def dq_slot(m, h):
         return dqt.at[m, pl.ds(h * HD, HD), :]
 
     for h in range(2):
-        norm = cl[h]
+        norm = jnp.sum(cl[h], axis=1, keepdims=True)
         out = (cacc[h] / norm).astype(BF16)
         o_cross[:, hs(h)] = out
         g = gcv[:, hs(h)]
-        lse = cm[h] + jnp.log(norm)
+        lse = mst[3, h] + jnp.log(norm)
         delta = jnp.sum(g.astype(F32) * out.astype(F32), axis=1, keepdims=True)
-        qt = cqt[hs(h)]
-        gt = gct[hs(h)]
-        dq = None
-        for k in range(8):
-            cols = slice(k * 2 * ROWS, (k + 1) * 2 * ROWS)
-            p = wst[h, :, cols] * jnp.exp(mst[k, h] - lse)
-            ds = (p * (dpst[h, :, cols] - delta) * SCALE).astype(BF16)
-            add = nt(ds, kvt[hs(h), cols])
-            dq = add if dq is None else dq + add
-            dkvt[h, 0:HD, cols] = nn(qt, ds).astype(BF16)
-            dkvt[h, HD:, cols] = nn(gt, p.astype(BF16)).astype(BF16)
+        for i, chunks in enumerate(groups):
+            fix = jnp.exp(mst[i, h] - lse)
+            for k in chunks:
+                cols = span(k)
+                p = wst[h, :, cols] * fix
+                prob[:, cols] = p.astype(BF16)
+                dscore[:, cols] = (p * (dpst[h, :, cols] - delta) * SCALE).astype(BF16)
+        dq = nt(dscore[...], kvt[hs(h), :])
         dqt[0, hs(h), :] = dq.astype(BF16).T
         for m in (4, 1, 3, 2):
             send(dq_slot(0, h), dq_slot(m, h), dq_sem.at[m, h], partner[m])
+        dkvt[h, 0:HD, :] = nn(cqt[hs(h)], dscore[...]).astype(BF16)
+        dkvt[h, HD:, :] = nn(gct[hs(h)], prob[...]).astype(BF16)
         piece = weight_part(h, 1 - xh).astype(BF16)
         for z in range(4):
             wmine[h, z] = piece[:, z * HD:(z + 1) * HD]
@@ -346,18 +346,6 @@
         arrived(dq_slot(4, h), dq_sem.at[4, h])
         for m in (1, 3, 2):
             send(dq_slot(4, h), dq_slot(4 + m, h), dq_sem.at[4 + m, h], partner[m])
-
-    forward_dq(0)
-    for h in range(2):
-        piece = weight_part(h, xh)
-        for z in range(4):
-            wown[h, z] = piece[:, z * HD:(z + 1) * HD]
-    for i, ee in enumerate((ydn, yup, yfar, sib)):
-        arrived(tb.at[pl.ds(1, 7), trange(ee)], tokg_sem.at[i])
-    for i, ee in enumerate((ydn, yup, yfar)):
-        spot = tb.at[pl.ds(1, 7), trange(ee)]
-        send(spot, spot, tsib_sem.at[i], dev["sib"])
-    forward_dq(1)
 
     def sum_and_pass(h):
         arrived(wpeer.at[h], wp_sem.at[h])
@@ -368,8 +356,49 @@
                 wpeer.at[h, partner[m][1] - 4 * xh], wz.at[m, h], wz_sem.at[m, h], partner[m]
             )
 
+    def own_weights(h):
+        piece = weight_part(h, xh)
+        for z in range(4):
+            wown[h, z] = piece[:, z * HD:(z + 1) * HD]
+
+    for m in range(1, 8):
+        arrived(tb.at[m, trows], tok_sem.at[m])
+    l_tb.wait()
+
+    def trange(ee):
+        return pl.ds(pl.multiple_of((ee // 4 * 2 + ee % 2) * 32, 32), 32)
+
+    moved = tb.at[pl.ds(1, 7), trows]
+    for i, name in enumerate(("yup", "ydn", "yfar", "sib")):
+        send(moved, moved, tokg_sem.at[i], dev[name])
+    forward_dq(0)
+    for m in (5, 6, 7):
+        arrived(blk.at[m], blk_sem.at[m])
+    lax.fori_loop(0, 4 * xh, self_scores, 0)
+    for h in range(2):
+        top = jnp.max(sm[h], axis=1, keepdims=True)
+        fix = jnp.exp(st_top[h] - top)
+        st_top[h] = top
+        sl[h] = sl[h] * fix
+        sacc[h] = sacc[h] * fix
+    lax.fori_loop(0, 4 * xh, self_weights, 0)
+    for h in range(2):
+        norm = jnp.sum(sl[h], axis=1, keepdims=True)
+        out = (sacc[h] / norm).astype(BF16)
+        o_self[:, hs(h)] = out
+        g = own[3, :, hs(h)]
+        lse = st_top[h] + jnp.log(norm)
+        delta = jnp.sum(g.astype(F32) * out.astype(F32), axis=1, keepdims=True)
+        sm[h] = jnp.broadcast_to(lse, (ROWS, HD))
+        sl[h] = jnp.broadcast_to(delta, (ROWS, HD))
+        stat[0, 2 * h:2 * h + 1, :] = sm[h].T[0:1]
+        stat[0, 2 * h + 1:2 * h + 2, :] = sl[h].T[0:1]
+    for m in range(1, 8):
+        send(stat.at[0], stat.at[m], stat_sem.at[m], partner[m])
+    own_weights(0)
+    own_weights(1)
     sum_and_pass(0)
-
+    forward_dq(1)
     def query_grad(h, s, v, k):
         p = jnp.exp(s - sm[h, :, 0:1])
         dp = nt(own[3, :, hs(h)], v)
@@ -394,12 +423,19 @@
         ds = (p * (dp - delta) * SCALE).astype(BF16)
         return nn(ds, q), nn(p.astype(BF16), g)
 
+    for i, ee in enumerate((ydn, yup, yfar, sib)):
+        arrived(tb.at[pl.ds(1, 7), trange(ee)], tokg_sem.at[i])
+    for i, ee in enumerate((ydn, yup, yfar)):
+        spot = tb.at[pl.ds(1, 7), trange(ee)]
+        send(spot, spot, tsib_sem.at[i], dev["sib"])
+
     for h in range(2):
         q, g = own[2, :, hs(h)], own[3, :, hs(h)]
         st = jnp.where(col >= row, nt(own[0, :, hs(h)], q) * SCALE, -1e30)
         dk, dv = key_grad(h, st, q, g, stat[0, 2 * h:2 * h + 1], stat[0, 2 * h + 1:2 * h + 2])
         o_dsk[:, hs(h)] = dk
         o_dsv[:, hs(h)] = dv
+    sum_and_pass(1)
     for m in range(1, 8):
         arrived(stat.at[m], stat_sem.at[m])
 
@@ -416,8 +452,6 @@
         return carry
 
     lax.fori_loop(d + 1, 8, self_key, 0)
-    sum_and_pass(1)
-
     for i, ee in enumerate((ydn, yup, yfar)):
         ss = ee + 1 - 2 * core
         arrived(tb.at[pl.ds(1, 7), trange(ss)], tsib_sem.at[i])
@@ -483,15 +517,18 @@
             pltpu.VMEM((512, 1024), BF16),
             pltpu.VMEM((4, 256, 256), BF16),
             pltpu.VMEM((256, 256), BF16),
-            pltpu.VMEM((8, 2, 256, 1024), BF16),
+            pltpu.VMEM((8, 2, 2, 128, 1024), BF16),
             pltpu.VMEM((512, 4096), BF16),
             pltpu.VMEM((2, 256, 4096), F32),
             pltpu.VMEM((2, 256, 4096), F32),
-            pltpu.VMEM((8, 2, 256, 1), F32),
+            pltpu.VMEM((4, 2, 256, 1), F32),
             pltpu.VMEM((2, 256, 4096), BF16),
+            pltpu.VMEM((256, 4096), BF16),
+            pltpu.VMEM((256, 4096), BF16),
+            pltpu.VMEM((2, 256, 128), F32),
+            pltpu.VMEM((2, 256, 128), F32),
+            pltpu.VMEM((2, 256, 128), F32),
             pltpu.VMEM((2, 256, 1), F32),
-            pltpu.VMEM((2, 256, 1), F32),
-            pltpu.VMEM((2, 256, 128), F32),
             pltpu.VMEM((8, 2, 256, 256), F32),
             pltpu.VMEM((2, 256, 128), F32),
             pltpu.VMEM((2, 256, 128), F32),

time: 73.1 us -> 70.6 us (0.966)
  Pallas kernels: 72.2 us -> 69.3 us
    pallas_call x1, Pallas kernels: 69.8 us -> 66.8 us  [body(): pl.pallas_call(kernel, out_shape=shapes, in_specs=[any_] * 10, out_specs=...]
where the time goes in v3:
time: 70.6 us; the launch traced here: 70.1 us
  Pallas kernels  69.3 us (98%)
  between operations  0.83 us (1%)
    pallas_call x1, Pallas kernels, body(): pl.pallas_call(kernel, out_shape=shapes, in_specs=[any_] * 10, out_specs=...  66.8 us
    pallas_call x1, Pallas kernels, body(): pl.pallas_call(hand_over, out_shape=shapes, in_specs=[any_] * 8, out_spec...  2.41 us

profile of v3, /device:TPU:0, one launch (start us, length us, event | category | flops | bytes accessed | tf_op | source)
XLA Modules:
  0.0 70.1 jit_solution(2563280266533462038)
XLA Ops:
  0.6 66.8 %layer.1 = (bf16[256,256]{1,0:T(8,128)(2,1)}, f32[256,256]{1,0:T(8,128)}, f32[256,256]{1,0:T(8,128)}, f32[256,256]{1,0:T(8,128)}, bf16[256,256]{1,0:T(8,128)(2,1...) custom-call(bf16[256,4096]{1,0:T(8,128)(2,1)} %tok_h.1, bf16[4096,256]{1,0:T(8,128)(2,1)} %wq_h.1, ...), custom_call_target="tpu_custom_call" | custom-call | tf_op jit(solution)/shard_map/layer/pallas_call | solution.py:508
  67.5 2.4 %hand_over.1 = (bf16[256,256]{1,0:T(8,128)(2,1)}, f32[256,256]{1,0:T(8,128)}, f32[256,256]{1,0:T(8,128)}, f32[256,256]{1,0:T(8,128)}, bf16[256,256]{1,0:T(8,128)...) custom-call(bf16[256,256]{1,0:T(8,128)(2,1)} %get-tuple-element.16.refs_0_, ...), custom_call_target="tpu_custom_call" | custom-call | tf_op jit(solution)/shard_map/hand_over/pallas_call | solution.py:552

commit v4 on v3

--- a/solution.py
+++ b/solution.py
@@ -104,8 +104,8 @@
     def share(k, i):
         send(part(k, i), part(k, i, 1), sib_sem.at[k, i], dev["sib"])
 
-    def shared(k):
-        for i in range(4):
+    def shared(k, pieces=range(4)):
+        for i in pieces:
             arrived(part(k, i, 1), sib_sem.at[k, i])
 
     for c in l_own:
@@ -160,8 +160,10 @@
             out = f(out, x[:, i * HD:(i + 1) * HD])
         return out
 
-    def cross_scores(k, first=False):
+    def cross_scores(k, first=False, half=None):
         cols = span(k)
+        if half is not None:
+            cols = slice(cols.start + half * ROWS, cols.start + (half + 1) * ROWS)
         x = ctx2[cols]
         kv = [nt(wkvt[i * ROWS:(i + 1) * ROWS], x).astype(BF16) for i in range(2)]
         for i in range(2):
@@ -171,7 +173,7 @@
             wst[h, :, cols] = s
             top = lanes(jnp.maximum, s)
             cm[h] = top if first else jnp.maximum(cm[h], top)
-            dpst[h, :, cols] = nn(gcv[:, hs(h)], kv[1][hs(h)])
+            dpst[h, :, cols] = nn(gcv[:, hs(h)], kv[1][hs(h)]) * SCALE
 
     def cross_weights(g, chunks):
         for h in range(2):
@@ -193,7 +195,7 @@
             cl[h] = add_l
             cacc[h] = add_o
 
-    groups = ((0, 1), (6, 2), (4, 7, 3), (5,))
+    groups = ((0, 1, 6, 2), (4, 7, 3), (5,))
 
     row = lax.broadcasted_iota(jnp.int32, (ROWS, ROWS), 0)
     col = lax.broadcasted_iota(jnp.int32, (ROWS, ROWS), 1)
@@ -248,17 +250,21 @@
     arrived(blk.at[4], blk_sem.at[4])
     for m in (1, 3, 2):
         blk_out(m, 4 + m, blk.at[4])
+    shared(6, (0, 1))
+    cross_scores(6, half=0)
     got_up(2)
     got_down(0)
+    shared(2, (2, 3))
+    cross_scores(2, half=1)
     got_up(3)
     got_down(1)
-    shared(6)
-    cross_scores(6)
+    shared(6, (2, 3))
+    cross_scores(6, half=1)
     for i in range(4):
         got(1, i)
         share(1, i)
-    shared(2)
-    cross_scores(2)
+    shared(2, (0, 1))
+    cross_scores(2, half=0)
     shared(1)
     cross_scores(1)
     for m in (1, 2, 3):
@@ -275,7 +281,8 @@
         got(4, i)
         share(4, i)
     cross_weights(0, groups[0])
-    cross_weights(1, groups[1])
+    shared(4)
+    cross_scores(4)
     for h in range(2):
         top = jnp.max(sm[h], axis=1, keepdims=True)
         st_top[h] = top
@@ -283,8 +290,6 @@
         sl[h] = halves(jnp.add, w)
         sacc[h] = nn(w.astype(BF16), own[1, :, hs(h)])
     lax.fori_loop(4 * xh, d, self_weights, 0)
-    shared(4)
-    cross_scores(4)
     for i in (0, 1):
         got(7, 2 + i)
         share(7, 2 + i)
@@ -306,41 +311,59 @@
     for m in range(1, 8):
         send(tok.at[trows, tcols(partner[m][1])], tb.at[m, trows], tok_sem.at[m], partner[m])
     l_tb = load(tok.at[:, tcols(d)], tb.at[0])
-    cross_weights(2, groups[2])
+    cross_weights(1, groups[1])
     shared(5)
     cross_scores(5)
-    cross_weights(3, groups[3])
+    cross_weights(2, groups[2])
 
     def weight_part(h, group):
         return nn(dkvt[h], ctx2[:, pl.ds(pl.multiple_of(group * 512, 512), 512)])
 
     def dq_slot(m, h):
         return dqt.at[m, pl.ds(h * HD, HD), :]
+
+    def trange(ee):
+        return pl.ds(pl.multiple_of((ee // 4 * 2 + ee % 2) * 32, 32), 32)
+
+    def gather_tokens():
+        for m in range(1, 8):
+            arrived(tb.at[m, trows], tok_sem.at[m])
+        l_tb.wait()
+        moved = tb.at[pl.ds(1, 7), trows]
+        for i, name in enumerate(("yup", "ydn", "yfar", "sib")):
+            send(moved, moved, tokg_sem.at[i], dev[name])
+
+    def peer_weights(h):
+        piece = weight_part(h, 1 - xh).astype(BF16)
+        for z in range(4):
+            wmine[h, z] = piece[:, z * HD:(z + 1) * HD]
+        for m in (2, 1, 3, 0):
+            spot = partner[m][1] - 4 * xh
+            send(wmine.at[h, spot], wpeer.at[h, spot], wp_sem.at[h, m], partner[4])
 
     for h in range(2):
         norm = jnp.sum(cl[h], axis=1, keepdims=True)
         out = (cacc[h] / norm).astype(BF16)
         o_cross[:, hs(h)] = out
         g = gcv[:, hs(h)]
-        lse = mst[3, h] + jnp.log(norm)
-        delta = jnp.sum(g.astype(F32) * out.astype(F32), axis=1, keepdims=True)
+        lse = mst[2, h] + jnp.log(norm)
+        delta = jnp.sum(g.astype(F32) * out.astype(F32), axis=1, keepdims=True) * SCALE
         for i, chunks in enumerate(groups):
             fix = jnp.exp(mst[i, h] - lse)
             for k in chunks:
                 cols = span(k)
                 p = wst[h, :, cols] * fix
                 prob[:, cols] = p.astype(BF16)
-                dscore[:, cols] = (p * (dpst[h, :, cols] - delta) * SCALE).astype(BF16)
+                dscore[:, cols] = (p * (dpst[h, :, cols] - delta)).astype(BF16)
         dq = nt(dscore[...], kvt[hs(h), :])
         dqt[0, hs(h), :] = dq.astype(BF16).T
         for m in (4, 1, 3, 2):
             send(dq_slot(0, h), dq_slot(m, h), dq_sem.at[m, h], partner[m])
         dkvt[h, 0:HD, :] = nn(cqt[hs(h)], dscore[...]).astype(BF16)
         dkvt[h, HD:, :] = nn(gct[hs(h)], prob[...]).astype(BF16)
-        piece = weight_part(h, 1 - xh).astype(BF16)
-        for z in range(4):
-            wmine[h, z] = piece[:, z * HD:(z + 1) * HD]
-        send(wmine.at[h], wpeer.at[h], wp_sem.at[h], partner[4])
+        if h == 0:
+            peer_weights(0)
+            gather_tokens()
 
     def forward_dq(h):
         arrived(dq_slot(4, h), dq_sem.at[4, h])
@@ -348,29 +371,17 @@
             send(dq_slot(4, h), dq_slot(4 + m, h), dq_sem.at[4 + m, h], partner[m])
 
     def sum_and_pass(h):
-        arrived(wpeer.at[h], wp_sem.at[h])
-        wown[h] = wown[h] + wpeer[h].astype(F32)
-        wpeer[h] = wown[h].astype(BF16)
-        for m in (1, 3, 2):
-            send(
-                wpeer.at[h, partner[m][1] - 4 * xh], wz.at[m, h], wz_sem.at[m, h], partner[m]
-            )
+        for m in (2, 1, 3):
+            spot = partner[m][1] - 4 * xh
+            arrived(wpeer.at[h, spot], wp_sem.at[h, m])
+            wpeer[h, spot] = (wown[h, spot] + wpeer[h, spot].astype(F32)).astype(BF16)
+            send(wpeer.at[h, spot], wz.at[m, h], wz_sem.at[m, h], partner[m])
 
     def own_weights(h):
         piece = weight_part(h, xh)
         for z in range(4):
             wown[h, z] = piece[:, z * HD:(z + 1) * HD]
 
-    for m in range(1, 8):
-        arrived(tb.at[m, trows], tok_sem.at[m])
-    l_tb.wait()
-
-    def trange(ee):
-        return pl.ds(pl.multiple_of((ee // 4 * 2 + ee % 2) * 32, 32), 32)
-
-    moved = tb.at[pl.ds(1, 7), trows]
-    for i, name in enumerate(("yup", "ydn", "yfar", "sib")):
-        send(moved, moved, tokg_sem.at[i], dev[name])
     forward_dq(0)
     for m in (5, 6, 7):
         arrived(blk.at[m], blk_sem.at[m])
@@ -395,6 +406,7 @@
         stat[0, 2 * h + 1:2 * h + 2, :] = sl[h].T[0:1]
     for m in range(1, 8):
         send(stat.at[0], stat.at[m], stat_sem.at[m], partner[m])
+    peer_weights(1)
     own_weights(0)
     own_weights(1)
     sum_and_pass(0)
@@ -423,12 +435,6 @@
         ds = (p * (dp - delta) * SCALE).astype(BF16)
         return nn(ds, q), nn(p.astype(BF16), g)
 
-    for i, ee in enumerate((ydn, yup, yfar, sib)):
-        arrived(tb.at[pl.ds(1, 7), trange(ee)], tokg_sem.at[i])
-    for i, ee in enumerate((ydn, yup, yfar)):
-        spot = tb.at[pl.ds(1, 7), trange(ee)]
-        send(spot, spot, tsib_sem.at[i], dev["sib"])
-
     for h in range(2):
         q, g = own[2, :, hs(h)], own[3, :, hs(h)]
         st = jnp.where(col >= row, nt(own[0, :, hs(h)], q) * SCALE, -1e30)
@@ -436,6 +442,12 @@
         o_dsk[:, hs(h)] = dk
         o_dsv[:, hs(h)] = dv
     sum_and_pass(1)
+    for i, ee in enumerate((ydn, yup, yfar, sib)):
+        arrived(tb.at[pl.ds(1, 7), trange(ee)], tokg_sem.at[i])
+    for i, ee in enumerate((ydn, yup, yfar)):
+        spot = tb.at[pl.ds(1, 7), trange(ee)]
+        send(spot, spot, tsib_sem.at[i], dev["sib"])
+
     for m in range(1, 8):
         arrived(stat.at[m], stat_sem.at[m])
 
@@ -468,7 +480,8 @@
             arrived(wz.at[m, h], wz_sem.at[m, h])
     mine = d - 4 * xh
     for h in range(2):
-        total = wown[h, mine]
+        arrived(wpeer.at[h, mine], wp_sem.at[h, 0])
+        total = wown[h, mine] + wpeer[h, mine].astype(F32)
         for m in (1, 2, 3):
             total = total + wz[m, h].astype(F32)
         o_gwk[:, hs(h)] = total[0:HD].T
@@ -542,7 +555,7 @@
             pltpu.VMEM((2, 4, 256, 128), BF16),
             pltpu.VMEM((4, 2, 256, 128), BF16),
             dma((16,)), dma((128,)), dma((8, 4)), dma((8, 4)), dma((8,)), dma((8,)), dma((8,)),
-            dma((4,)), dma((3,)), dma((8, 2)), dma((2,)), dma((4, 2)),
+            dma((4,)), dma((3,)), dma((8, 2)), dma((2, 4)), dma((4, 2)),
         ],
         compiler_params=pltpu.CompilerParams(
             collective_id=0, has_side_effects=True, vmem_limit_bytes=62 << 20

time: 70.6 us -> 67.9 us (0.962)
  Pallas kernels: 69.3 us -> 66.9 us
    pallas_call x1, Pallas kernels: 66.8 us -> 64.5 us  [body(): pl.pallas_call(kernel, out_shape=shapes, in_specs=[any_] * 10, out_specs=...]
where the time goes in v4:
time: 67.9 us; the launch traced here: 67.7 us
  Pallas kernels  66.9 us (99%)
  between operations  0.83 us (1%)
    pallas_call x1, Pallas kernels, body(): pl.pallas_call(kernel, out_shape=shapes, in_specs=[any_] * 10, out_specs=...  64.5 us
    pallas_call x1, Pallas kernels, body(): pl.pallas_call(hand_over, out_shape=shapes, in_specs=[any_] * 8, out_spec...  2.41 us

profile of v4, /device:TPU:0, one launch (start us, length us, event | category | flops | bytes accessed | tf_op | source)
XLA Modules:
  0.0 67.7 jit_solution(2876109596094524766)
XLA Ops:
  0.6 64.5 %layer.1 = (bf16[256,256]{1,0:T(8,128)(2,1)}, f32[256,256]{1,0:T(8,128)}, f32[256,256]{1,0:T(8,128)}, f32[256,256]{1,0:T(8,128)}, bf16[256,256]{1,0:T(8,128)(2,1...) custom-call(bf16[256,4096]{1,0:T(8,128)(2,1)} %tok_h.1, bf16[4096,256]{1,0:T(8,128)(2,1)} %wq_h.1, ...), custom_call_target="tpu_custom_call" | custom-call | tf_op jit(solution)/shard_map/layer/pallas_call | solution.py:521
  65.1 2.4 %hand_over.1 = (bf16[256,256]{1,0:T(8,128)(2,1)}, f32[256,256]{1,0:T(8,128)}, f32[256,256]{1,0:T(8,128)}, f32[256,256]{1,0:T(8,128)}, bf16[256,256]{1,0:T(8,128)...) custom-call(bf16[256,256]{1,0:T(8,128)(2,1)} %get-tuple-element.16.refs_0_, ...), custom_call_target="tpu_custom_call" | custom-call | tf_op jit(solution)/shard_map/hand_over/pallas_call | solution.py:565

commit v5 on v4

--- a/solution.py
+++ b/solution.py
@@ -1,3 +1,5 @@
+import math
+
 import jax
 import jax.numpy as jnp
 from jax import lax
@@ -23,11 +25,11 @@
 
 def kernel(
     tok_h, wq_h, ctx_h, wk_h, wv_h, sq_h, sk_h, sv_h, gs_h, gc_h,
+    r_self, r_dsq, r_dsk, r_dsv, r_cross, r_gwq, r_gwk, r_gwv,
     o_self, o_dsq, o_dsk, o_dsv, o_cross, o_gwq, o_gwk, o_gwv,
     tok, wq, wkv, wkvt, own, gc, ctx, kvt, wst, dpst, mst, dkvt,
     prob, dscore, cm, cl, cacc, st_top, sst, sm, sl, sacc, blk, stat, tb, dqt, wown, wmine, wpeer, wz,
-    lsem, ssem, ctx_sem, sib_sem, blk_sem, stat_sem, tok_sem, tokg_sem, tsib_sem, dq_sem, wp_sem,
-    wz_sem,
+    lsem, ssem, ctx_sem, sib_sem, blk_sem, stat_sem, tok_sem, dq_sem, wp_sem, wz_sem, out_sem,
 ):
     e = lax.axis_index("enc")
     d = lax.axis_index("dec")
@@ -74,15 +76,29 @@
     l_tok = load(tok_h, tok)
     l_wq = load(wq_h, wq)
 
-    sends = []
-
-    def send(src, dst, rsem, target):
-        copy = pltpu.make_async_remote_copy(
-            src_ref=src, dst_ref=dst, send_sem=ssem.at[len(sends)], recv_sem=rsem,
+    leaving = []
+
+    def store(src, dst):
+        copy = pltpu.make_async_copy(src, dst, out_sem.at[len(leaving)])
+        copy.start()
+        leaving.append(copy)
+
+    sent = {}
+
+    def send(kind, src, dst, rsem, target):
+        group = list(sent).index(kind) if kind in sent else len(sent)
+        pltpu.make_async_remote_copy(
+            src_ref=src, dst_ref=dst, send_sem=ssem.at[group], recv_sem=rsem,
             device_id=target, device_id_type=MESH,
-        )
-        copy.start()
-        sends.append(copy)
+        ).start()
+        sent[kind] = sent.get(kind, 0) + math.prod(src.shape)
+
+    def sent_all(kind, whole):
+        assert sent[kind] == math.prod(whole.shape), kind
+        pltpu.make_async_remote_copy(
+            src_ref=whole, dst_ref=whole, send_sem=ssem.at[list(sent).index(kind)],
+            recv_sem=lsem.at[0], device_id=dev["sib"], device_id_type=MESH,
+        ).wait_send()
 
     def arrived(dst, rsem):
         pltpu.make_async_remote_copy(
@@ -91,22 +107,37 @@
         ).wait_recv()
 
     quarter = ROWS // 4
+    slots = {}
+
+    def slot_sem(k, i):
+        alone = k in (2, 6) or (k, i) in ((7, 0), (7, 1), (3, 2), (3, 3))
+        return ctx_sem.at[slots.setdefault((k, i if alone else i // 2 * 2), len(slots))]
 
     def part(k, i, side=0):
         return ctx.at[k, i // 2, side, pl.ds(i % 2 * quarter, quarter), :]
 
+    def pair(k, a, side=0):
+        return ctx.at[k, a, side]
+
     def pass_on(src, k, i, target):
-        send(src, part(k, i), ctx_sem.at[k, i], target)
+        send("context", src, part(k, i), slot_sem(k, i), target)
 
     def got(k, i):
-        arrived(part(k, i), ctx_sem.at[k, i])
+        arrived(part(k, i), slot_sem(k, i))
+
+    def got_pair(k, a):
+        arrived(pair(k, a), slot_sem(k, 2 * a))
+        share_pair(k, a)
 
     def share(k, i):
-        send(part(k, i), part(k, i, 1), sib_sem.at[k, i], dev["sib"])
-
-    def shared(k, pieces=range(4)):
-        for i in pieces:
-            arrived(part(k, i, 1), sib_sem.at[k, i])
+        send("share", part(k, i), part(k, i, 1), sib_sem.at[2 * k + i // 2], dev["sib"])
+
+    def share_pair(k, a):
+        send("share", pair(k, a), pair(k, a, 1), sib_sem.at[2 * k + a], dev["sib"])
+
+    def shared(k, halves_=(0, 1)):
+        for a in halves_:
+            arrived(pair(k, a, 1), sib_sem.at[2 * k + a])
 
     for c in l_own:
         c.wait()
@@ -119,16 +150,16 @@
         return own.at[pl.ds(2 * bit, 2)]
 
     def blk_out(m, slot, src):
-        send(src, blk.at[slot], blk_sem.at[slot], partner[m])
+        spot = 1 if slot == 4 else 0 if slot < 4 else 2
+        send("block", src, blk.at[slot], blk_sem.at[spot], partner[m])
 
     blk_out(4, 4, own_block(4))
     for i in (0, 1):
-        pass_on(part(0, i), 1, i, dev["xi"])
-        pass_on(part(0, 2 + i), 1, 2 + i, dev["xo"])
+        send("context", pair(0, i), pair(1, i), slot_sem(1, 2 * i), dev["xo" if i else "xi"])
         pass_on(part(0, i), 6, i, dev["yup"])
         pass_on(part(0, 2 + i), 2, 2 + i, dev["ydn"])
-    for i in range(4):
-        share(0, i)
+    for a in range(2):
+        share_pair(0, a)
     for i in (0, 1):
         pass_on(part(0, 2 + i), 6, 2 + i, dev["yup"])
         pass_on(part(0, i), 2, i, dev["ydn"])
@@ -160,10 +191,11 @@
             out = f(out, x[:, i * HD:(i + 1) * HD])
         return out
 
+    def unit(k, half):
+        return slice((2 * k + half) * ROWS, (2 * k + half + 1) * ROWS)
+
     def cross_scores(k, first=False, half=None):
-        cols = span(k)
-        if half is not None:
-            cols = slice(cols.start + half * ROWS, cols.start + (half + 1) * ROWS)
+        cols = span(k) if half is None else unit(k, half)
         x = ctx2[cols]
         kv = [nt(wkvt[i * ROWS:(i + 1) * ROWS], x).astype(BF16) for i in range(2)]
         for i in range(2):
@@ -180,8 +212,7 @@
             top = jnp.max(cm[h], axis=1, keepdims=True)
             mst[g, h] = top
             add_l, add_o = None, None
-            for k in chunks:
-                cols = span(k)
+            for cols in chunks:
                 w = jnp.exp(wst[h, :, cols] - top)
                 wst[h, :, cols] = w
                 one_l = lanes(jnp.add, w)
@@ -195,7 +226,11 @@
             cl[h] = add_l
             cacc[h] = add_o
 
-    groups = ((0, 1, 6, 2), (4, 7, 3), (5,))
+    groups = (
+        (span(0), span(1), span(6), span(2)),
+        (span(4), unit(7, 0), unit(3, 1)),
+        (unit(7, 1), unit(3, 0), span(5)),
+    )
 
     row = lax.broadcasted_iota(jnp.int32, (ROWS, ROWS), 0)
     col = lax.broadcasted_iota(jnp.int32, (ROWS, ROWS), 1)
@@ -247,28 +282,26 @@
         sm[h] = halves(jnp.maximum, s)
     got_up(1)
     got_down(3)
-    arrived(blk.at[4], blk_sem.at[4])
+    arrived(blk.at[4], blk_sem.at[1])
     for m in (1, 3, 2):
         blk_out(m, 4 + m, blk.at[4])
-    shared(6, (0, 1))
+    shared(6, (0,))
     cross_scores(6, half=0)
     got_up(2)
     got_down(0)
-    shared(2, (2, 3))
+    shared(2, (1,))
     cross_scores(2, half=1)
     got_up(3)
     got_down(1)
-    shared(6, (2, 3))
+    shared(6, (1,))
     cross_scores(6, half=1)
-    for i in range(4):
-        got(1, i)
-        share(1, i)
-    shared(2, (0, 1))
+    for a in range(2):
+        got_pair(1, a)
+    shared(2, (0,))
     cross_scores(2, half=0)
     shared(1)
     cross_scores(1)
-    for m in (1, 2, 3):
-        arrived(blk.at[m], blk_sem.at[m])
+    arrived(blk.at[pl.ds(1, 3)], blk_sem.at[0])
     lax.fori_loop(4 * xh, d, self_scores, 0)
     for i in (0, 1):
         got(7, i)
@@ -277,12 +310,18 @@
         got(3, 2 + i)
         pass_on(part(3, 2 + i), 5, 2 + i, dev["ydn"])
         share(3, 2 + i)
-    for i in range(4):
-        got(4, i)
-        share(4, i)
+    for a in range(2):
+        got_pair(4, a)
     cross_weights(0, groups[0])
+    shared(7, (0,))
+    cross_scores(7, half=0)
+    shared(3, (1,))
+    cross_scores(3, half=1)
     shared(4)
     cross_scores(4)
+    cross_weights(1, groups[1])
+    got_pair(7, 1)
+    got_pair(3, 0)
     for h in range(2):
         top = jnp.max(sm[h], axis=1, keepdims=True)
         st_top[h] = top
@@ -290,18 +329,12 @@
         sl[h] = halves(jnp.add, w)
         sacc[h] = nn(w.astype(BF16), own[1, :, hs(h)])
     lax.fori_loop(4 * xh, d, self_weights, 0)
-    for i in (0, 1):
-        got(7, 2 + i)
-        share(7, 2 + i)
-        got(3, i)
-        share(3, i)
-    shared(7)
-    cross_scores(7)
-    for i in range(4):
-        got(5, i)
-        share(5, i)
-    shared(3)
-    cross_scores(3)
+    for a in range(2):
+        got_pair(5, a)
+    shared(7, (1,))
+    cross_scores(7, half=1)
+    shared(3, (0,))
+    cross_scores(3, half=0)
     lane = (y * 2 + core) * 32
     trows = pl.ds(pl.multiple_of(lane, 32), 32)
 
@@ -309,9 +342,8 @@
         return pl.ds(pl.multiple_of(p * 512, 512), 512)
 
     for m in range(1, 8):
-        send(tok.at[trows, tcols(partner[m][1])], tb.at[m, trows], tok_sem.at[m], partner[m])
+        send("columns", tok.at[trows, tcols(partner[m][1])], tb.at[m, trows], tok_sem.at[0], partner[m])
     l_tb = load(tok.at[:, tcols(d)], tb.at[0])
-    cross_weights(1, groups[1])
     shared(5)
     cross_scores(5)
     cross_weights(2, groups[2])
@@ -326,20 +358,22 @@
         return pl.ds(pl.multiple_of((ee // 4 * 2 + ee % 2) * 32, 32), 32)
 
     def gather_tokens():
-        for m in range(1, 8):
-            arrived(tb.at[m, trows], tok_sem.at[m])
+        moved = tb.at[pl.ds(1, 7), trows]
+        arrived(moved, tok_sem.at[0])
         l_tb.wait()
-        moved = tb.at[pl.ds(1, 7), trows]
-        for i, name in enumerate(("yup", "ydn", "yfar", "sib")):
-            send(moved, moved, tokg_sem.at[i], dev[name])
+        for name in ("yup", "ydn", "yfar", "sib"):
+            send("rows", moved, moved, tok_sem.at[1], dev[name])
+
+    def send_pieces(h, pieces):
+        for m in pieces:
+            spot = partner[m][1] - 4 * xh
+            send("peer", wmine.at[h, spot], wpeer.at[h, spot], wp_sem.at[h, m], partner[4])
 
     def peer_weights(h):
         piece = weight_part(h, 1 - xh).astype(BF16)
         for z in range(4):
             wmine[h, z] = piece[:, z * HD:(z + 1) * HD]
-        for m in (2, 1, 3, 0):
-            spot = partner[m][1] - 4 * xh
-            send(wmine.at[h, spot], wpeer.at[h, spot], wp_sem.at[h, m], partner[4])
+        send_pieces(h, (2, 1, 3))
 
     for h in range(2):
         norm = jnp.sum(cl[h], axis=1, keepdims=True)
@@ -350,15 +384,14 @@
         delta = jnp.sum(g.astype(F32) * out.astype(F32), axis=1, keepdims=True) * SCALE
         for i, chunks in enumerate(groups):
             fix = jnp.exp(mst[i, h] - lse)
-            for k in chunks:
-                cols = span(k)
+            for cols in chunks:
                 p = wst[h, :, cols] * fix
                 prob[:, cols] = p.astype(BF16)
                 dscore[:, cols] = (p * (dpst[h, :, cols] - delta)).astype(BF16)
         dq = nt(dscore[...], kvt[hs(h), :])
         dqt[0, hs(h), :] = dq.astype(BF16).T
         for m in (4, 1, 3, 2):
-            send(dq_slot(0, h), dq_slot(m, h), dq_sem.at[m, h], partner[m])
+            send("dq", dq_slot(0, h), dq_slot(m, h), dq_sem.at[h if m == 4 else 2], partner[m])
         dkvt[h, 0:HD, :] = nn(cqt[hs(h)], dscore[...]).astype(BF16)
         dkvt[h, HD:, :] = nn(gct[hs(h)], prob[...]).astype(BF16)
         if h == 0:
@@ -366,25 +399,26 @@
             gather_tokens()
 
     def forward_dq(h):
-        arrived(dq_slot(4, h), dq_sem.at[4, h])
+        arrived(dq_slot(4, h), dq_sem.at[h])
         for m in (1, 3, 2):
-            send(dq_slot(4, h), dq_slot(4 + m, h), dq_sem.at[4 + m, h], partner[m])
+            send("dq", dq_slot(4, h), dq_slot(4 + m, h), dq_sem.at[3], partner[m])
 
     def sum_and_pass(h):
         for m in (2, 1, 3):
             spot = partner[m][1] - 4 * xh
             arrived(wpeer.at[h, spot], wp_sem.at[h, m])
             wpeer[h, spot] = (wown[h, spot] + wpeer[h, spot].astype(F32)).astype(BF16)
-            send(wpeer.at[h, spot], wz.at[m, h], wz_sem.at[m, h], partner[m])
+            send("sum", wpeer.at[h, spot], wz.at[m, h], wz_sem.at[0], partner[m])
 
     def own_weights(h):
         piece = weight_part(h, xh)
         for z in range(4):
             wown[h, z] = piece[:, z * HD:(z + 1) * HD]
 
+    peer_weights(1)
     forward_dq(0)
-    for m in (5, 6, 7):
-        arrived(blk.at[m], blk_sem.at[m])
+    own_weights(0)
+    arrived(blk.at[pl.ds(5, 3)], blk_sem.at[2])
     lax.fori_loop(0, 4 * xh, self_scores, 0)
     for h in range(2):
         top = jnp.max(sm[h], axis=1, keepdims=True)
@@ -404,12 +438,14 @@
         sl[h] = jnp.broadcast_to(delta, (ROWS, HD))
         stat[0, 2 * h:2 * h + 1, :] = sm[h].T[0:1]
         stat[0, 2 * h + 1:2 * h + 2, :] = sl[h].T[0:1]
+    store(o_self, r_self)
+    store(o_cross, r_cross)
     for m in range(1, 8):
-        send(stat.at[0], stat.at[m], stat_sem.at[m], partner[m])
-    peer_weights(1)
-    own_weights(0)
+        send("stat", stat.at[0], stat.at[m], stat_sem.at[0], partner[m])
+    for h in range(2):
+        send_pieces(h, (0,))
+    sum_and_pass(0)
     own_weights(1)
-    sum_and_pass(0)
     forward_dq(1)
     def query_grad(h, s, v, k):
         p = jnp.exp(s - sm[h, :, 0:1])
@@ -428,6 +464,13 @@
         return carry
 
     lax.fori_loop(0, d, self_query, 0)
+    store(o_dsq, r_dsq)
+
+    sum_and_pass(1)
+    arrived(tb.at[pl.ds(1, 7), pl.ds(0, 128)], tok_sem.at[1])
+    for ee in (ydn, yup, yfar):
+        spot = tb.at[pl.ds(1, 7), trange(ee)]
+        send("rows", spot, spot, tok_sem.at[2], dev["sib"])
 
     def key_grad(h, st, q, g, lse, delta):
         p = jnp.exp(st - lse)
@@ -441,15 +484,7 @@
         dk, dv = key_grad(h, st, q, g, stat[0, 2 * h:2 * h + 1], stat[0, 2 * h + 1:2 * h + 2])
         o_dsk[:, hs(h)] = dk
         o_dsv[:, hs(h)] = dv
-    sum_and_pass(1)
-    for i, ee in enumerate((ydn, yup, yfar, sib)):
-        arrived(tb.at[pl.ds(1, 7), trange(ee)], tokg_sem.at[i])
-    for i, ee in enumerate((ydn, yup, yfar)):
-        spot = tb.at[pl.ds(1, 7), trange(ee)]
-        send(spot, spot, tsib_sem.at[i], dev["sib"])
-
-    for m in range(1, 8):
-        arrived(stat.at[m], stat_sem.at[m])
+    arrived(stat.at[pl.ds(1, 7)], stat_sem.at[0])
 
     def self_key(p, carry):
         slot = xor_slot(p)
@@ -464,20 +499,18 @@
         return carry
 
     lax.fori_loop(d + 1, 8, self_key, 0)
-    for i, ee in enumerate((ydn, yup, yfar)):
-        ss = ee + 1 - 2 * core
-        arrived(tb.at[pl.ds(1, 7), trange(ss)], tsib_sem.at[i])
-    for m in (1, 2, 3, 5, 6, 7):
-        for h in range(2):
-            arrived(dq_slot(m, h), dq_sem.at[m, h])
+    store(o_dsk, r_dsk)
+    store(o_dsv, r_dsv)
+    arrived(tb.at[pl.ds(1, 7), pl.ds(0, 96)], tok_sem.at[2])
+    arrived(dqt.at[pl.ds(1, 3)], dq_sem.at[2])
+    arrived(dqt.at[pl.ds(5, 3)], dq_sem.at[3])
     gw = None
     for m in range(8):
         add = nn(dqt[m], tb[m])
         gw = add if gw is None else gw + add
     o_gwq[...] = gw.T
-    for m in (1, 2, 3):
-        for h in range(2):
-            arrived(wz.at[m, h], wz_sem.at[m, h])
+    store(o_gwq, r_gwq)
+    arrived(wz.at[pl.ds(1, 3)], wz_sem.at[0])
     mine = d - 4 * xh
     for h in range(2):
         arrived(wpeer.at[h, mine], wp_sem.at[h, 0])
@@ -486,9 +519,20 @@
             total = total + wz[m, h].astype(F32)
         o_gwk[:, hs(h)] = total[0:HD].T
         o_gwv[:, hs(h)] = total[HD:].T
-
-    for copy in sends:
-        copy.wait_send()
+    store(o_gwk, r_gwk)
+    store(o_gwv, r_gwv)
+
+    sent_all("context", ctx.at[pl.ds(0, 7), :, 0])
+    sent_all("share", ctx.at[:, :, 0])
+    sent_all("block", blk.at[pl.ds(0, 7)])
+    sent_all("columns", tb.at[pl.ds(1, 7), pl.ds(0, 32)])
+    sent_all("rows", tb.at[pl.ds(1, 7), pl.ds(0, 224)])
+    sent_all("peer", wmine)
+    sent_all("dq", dqt.at[pl.ds(0, 7)])
+    sent_all("sum", wz.at[pl.ds(1, 3)])
+    sent_all("stat", stat.at[pl.ds(1, 7)])
+    for copy in leaving:
+        copy.wait()
 
 
 def hand_over(*refs):
@@ -509,7 +553,7 @@
 
 
 def body(*args):
-    vm, any_ = pl.BlockSpec(memory_space=pltpu.VMEM), pl.BlockSpec(memory_space=pl.ANY)
+    any_ = pl.BlockSpec(memory_space=pl.ANY)
     shape = jax.ShapeDtypeStruct
     block = (ROWS, ROWS)
     dma = pltpu.SemaphoreType.DMA
@@ -522,8 +566,8 @@
         kernel,
         out_shape=shapes,
         in_specs=[any_] * 10,
-        out_specs=[vm] * 8,
-        scratch_shapes=[
+        out_specs=[any_] * 8,
+        scratch_shapes=[pltpu.VMEM(x.shape, x.dtype) for x in shapes] + [
             pltpu.VMEM((256, 4096), BF16),
             pltpu.VMEM((4096, 256), BF16),
             pltpu.VMEM((1024, 512), BF16),
@@ -554,8 +598,8 @@
             pltpu.VMEM((2, 4, 256, 128), BF16),
             pltpu.VMEM((2, 4, 256, 128), BF16),
             pltpu.VMEM((4, 2, 256, 128), BF16),
-            dma((16,)), dma((128,)), dma((8, 4)), dma((8, 4)), dma((8,)), dma((8,)), dma((8,)),
-            dma((4,)), dma((3,)), dma((8, 2)), dma((2, 4)), dma((4, 2)),
+            dma((12,)), dma((9,)), dma((20,)), dma((16,)), dma((3,)), dma((1,)), dma((3,)),
+            dma((4,)), dma((2, 4)), dma((1,)), dma((8,)),
         ],
         compiler_params=pltpu.CompilerParams(
             collective_id=0, has_side_effects=True, vmem_limit_bytes=62 << 20

time: 67.9 us -> 65.5 us (0.965)
  Pallas kernels: 66.9 us -> 64.2 us
    pallas_call x1, Pallas kernels: 64.5 us -> 61.7 us  [body(): pl.pallas_call(kernel, out_shape=shapes, in_specs=[any_] * 10, out_specs=...]
where the time goes in v5:
time: 65.5 us; the launch traced here: 65 us
  Pallas kernels  64.2 us (98%)
  between operations  0.81 us (1%)
    pallas_call x1, Pallas kernels, body(): pl.pallas_call(kernel, out_shape=shapes, in_specs=[any_] * 10, out_specs=...  61.7 us
    pallas_call x1, Pallas kernels, body(): pl.pallas_call(hand_over, out_shape=shapes, in_specs=[any_] * 8, out_spec...  2.41 us

profile of v5, /device:TPU:0, one launch (start us, length us, event | category | flops | bytes accessed | tf_op | source)
XLA Modules:
  0.0 65.0 jit_solution(3505764133998052272)
XLA Ops:
  0.6 61.7 %layer.1 = (bf16[256,256]{1,0:T(8,128)(2,1)}, f32[256,256]{1,0:T(8,128)}, f32[256,256]{1,0:T(8,128)}, f32[256,256]{1,0:T(8,128)}, bf16[256,256]{1,0:T(8,128)(2,1...) custom-call(bf16[256,4096]{1,0:T(8,128)(2,1)} %tok_h.1, bf16[4096,256]{1,0:T(8,128)(2,1)} %wq_h.1, ...), custom_call_target="tpu_custom_call" | custom-call | tf_op jit(solution)/shard_map/layer/pallas_call | solution.py:565
  62.4 2.4 %hand_over.1 = (bf16[256,256]{1,0:T(8,128)(2,1)}, f32[256,256]{1,0:T(8,128)}, f32[256,256]{1,0:T(8,128)}, f32[256,256]{1,0:T(8,128)}, bf16[256,256]{1,0:T(8,128)...) custom-call(bf16[256,256]{1,0:T(8,128)(2,1)} %get-tuple-element.16.refs_0_, ...), custom_call_target="tpu_custom_call" | custom-call | tf_op jit(solution)/shard_map/hand_over/pallas_call | solution.py:609

commit v6 on v5

--- a/solution.py
+++ b/solution.py
@@ -155,7 +155,6 @@
 
     blk_out(4, 4, own_block(4))
     for i in (0, 1):
-        send("context", pair(0, i), pair(1, i), slot_sem(1, 2 * i), dev["xo" if i else "xi"])
         pass_on(part(0, i), 6, i, dev["yup"])
         pass_on(part(0, 2 + i), 2, 2 + i, dev["ydn"])
     for a in range(2):
@@ -227,8 +226,8 @@
             cacc[h] = add_o
 
     groups = (
-        (span(0), span(1), span(6), span(2)),
-        (span(4), unit(7, 0), unit(3, 1)),
+        (span(0), span(6), span(2)),
+        (span(1), span(4), unit(7, 0), unit(3, 1)),
         (unit(7, 1), unit(3, 0), span(5)),
     )
 
@@ -282,6 +281,8 @@
         sm[h] = halves(jnp.maximum, s)
     got_up(1)
     got_down(3)
+    for i in range(2):
+        send("context", pair(0, i), pair(1, i), slot_sem(1, 2 * i), dev["xo" if i else "xi"])
     arrived(blk.at[4], blk_sem.at[1])
     for m in (1, 3, 2):
         blk_out(m, 4 + m, blk.at[4])
@@ -295,14 +296,8 @@
     got_down(1)
     shared(6, (1,))
     cross_scores(6, half=1)
-    for a in range(2):
-        got_pair(1, a)
     shared(2, (0,))
     cross_scores(2, half=0)
-    shared(1)
-    cross_scores(1)
-    arrived(blk.at[pl.ds(1, 3)], blk_sem.at[0])
-    lax.fori_loop(4 * xh, d, self_scores, 0)
     for i in (0, 1):
         got(7, i)
         pass_on(part(7, i), 5, i, dev["yup"])
@@ -310,18 +305,17 @@
         got(3, 2 + i)
         pass_on(part(3, 2 + i), 5, 2 + i, dev["ydn"])
         share(3, 2 + i)
-    for a in range(2):
-        got_pair(4, a)
-    cross_weights(0, groups[0])
+    arrived(blk.at[pl.ds(1, 3)], blk_sem.at[0])
+    lax.fori_loop(4 * xh, d, self_scores, 0)
     shared(7, (0,))
     cross_scores(7, half=0)
     shared(3, (1,))
     cross_scores(3, half=1)
-    shared(4)
-    cross_scores(4)
-    cross_weights(1, groups[1])
-    got_pair(7, 1)
-    got_pair(3, 0)
+    cross_weights(0, groups[0])
+    for a in range(2):
+        got_pair(1, a)
+    for a in range(2):
+        got_pair(4, a)
     for h in range(2):
         top = jnp.max(sm[h], axis=1, keepdims=True)
         st_top[h] = top
@@ -329,6 +323,13 @@
         sl[h] = halves(jnp.add, w)
         sacc[h] = nn(w.astype(BF16), own[1, :, hs(h)])
     lax.fori_loop(4 * xh, d, self_weights, 0)
+    shared(1)
+    cross_scores(1)
+    shared(4)
+    cross_scores(4)
+    cross_weights(1, groups[1])
+    got_pair(7, 1)
+    got_pair(3, 0)
     for a in range(2):
         got_pair(5, a)
     shared(7, (1,))

time: 65.5 us -> 65.2 us (level)
  no operation moved by 1% of the time
where the time goes in v6:
time: 65.2 us; the launch traced here: 64.9 us
  Pallas kernels  64 us (98%)
  between operations  0.83 us (1%)
    pallas_call x1, Pallas kernels, body(): pl.pallas_call(kernel, out_shape=shapes, in_specs=[any_] * 10, out_specs=...  61.6 us
    pallas_call x1, Pallas kernels, body(): pl.pallas_call(hand_over, out_shape=shapes, in_specs=[any_] * 8, out_spec...  2.41 us

profile of v6, /device:TPU:0, one launch (start us, length us, event | category | flops | bytes accessed | tf_op | source)
XLA Modules:
  0.0 64.9 jit_solution(4637783525232084496)
XLA Ops:
  0.6 61.6 %layer.1 = (bf16[256,256]{1,0:T(8,128)(2,1)}, f32[256,256]{1,0:T(8,128)}, f32[256,256]{1,0:T(8,128)}, f32[256,256]{1,0:T(8,128)}, bf16[256,256]{1,0:T(8,128)(2,1...) custom-call(bf16[256,4096]{1,0:T(8,128)(2,1)} %tok_h.1, bf16[4096,256]{1,0:T(8,128)(2,1)} %wq_h.1, ...), custom_call_target="tpu_custom_call" | custom-call | tf_op jit(solution)/shard_map/layer/pallas_call | solution.py:566
  62.3 2.4 %hand_over.1 = (bf16[256,256]{1,0:T(8,128)(2,1)}, f32[256,256]{1,0:T(8,128)}, f32[256,256]{1,0:T(8,128)}, f32[256,256]{1,0:T(8,128)}, bf16[256,256]{1,0:T(8,128)...) custom-call(bf16[256,256]{1,0:T(8,128)(2,1)} %get-tuple-element.16.refs_0_, ...), custom_call_target="tpu_custom_call" | custom-call | tf_op jit(solution)/shard_map/hand_over/pallas_call | solution.py:610
